TPU v7x, 128 devices: a whole 4x4x4 slice. The times are simulated.
128 devices in a mesh: dp: 16 (over x, z_hi, core), tensor: 8 (over y, z_lo).
Axes of the slice: x: 4, y: 4, z: 4 (z_hi: 2, z_lo: 2; z = z_hi * 2 + z_lo), core: 2. Of those that a mesh axis runs over, the one named last changes fastest.
Arguments:
- activations: bfloat16 [6144, 4096], P('dp', 'tensor'), may hold values from -6 to 6
- out_grads: bfloat16 [6144, 16384], P('dp', 'tensor'), may hold values from -6 to 6
- basis_in: bfloat16 [4, 1024, 1024], replicated, may hold values from -0.1875 to 0.1875
- basis_out: bfloat16 [16, 1024, 1024], P('tensor'), may hold values from -0.1875 to 0.1875
Outputs:
- scales: float32 [4096, 16384], P('dp', 'tensor')
- natural: bfloat16 [4096, 16384], P('dp', 'tensor')
All inputs are finite; a program needn't handle non-finite values.
Results may differ from a plain program's by a relative error of at most 0.015.
Values may be sent and summed in bfloat16 or wider, within the bound.
No kernel may reach another device: no remote copies, remote signals or barrier semaphores. Data moves between devices by JAX's collectives and lax.ppermute only.
A program may use at most 192 MiB of HBM per device.

v0:
```python
import math

import jax
import jax.numpy as jnp
from jax import lax
from jax.experimental import pallas as pl
from jax.experimental.pallas import tpu as pltpu
from jax.sharding import Mesh
from jax.sharding import PartitionSpec as P

damping = 0.1


def along_y(v, d):
    return lax.ppermute(v, "y", [(i, (i + d) % 4) for i in range(4)])


def swap(v, axis):
    return lax.ppermute(v, axis, [(0, 1), (1, 0)])


def transpose_xy(v):
    return lax.ppermute(v, ("x", "y"), [(x * 4 + y, y * 4 + x) for x in range(4) for y in range(4)])


def squared(values):
    return values * values


def dot(left, right, contract=((1,), (0,))):
    return lax.dot_general(left, right, (contract, ((), ())), preferred_element_type=jnp.float32)


def fence(*values):
    return lax.optimization_barrier(values)


brief = pl.CostEstimate(flops=1, bytes_accessed=1, transcendentals=0)


def limit(mib):
    return pltpu.CompilerParams(vmem_limit_bytes=mib * 1024 * 1024)


def rotate_kernel(basis, first, second, out):
    tokens = first.shape[0]
    ways = ((1,), (1,))
    out[:, :tokens] = dot(basis[...], first[...], ways).astype(out.dtype)
    out[:, tokens:] = dot(basis[...], second[...], ways).astype(out.dtype)


def rotated(basis, first, second, side):
    tokens, depth = first.shape
    near = basis.shape[0] // 2
    tile = near // 2
    whole = pl.BlockSpec((tokens, depth), lambda i: (0, 0))
    return pl.pallas_call(
        rotate_kernel,
        grid=(2,),
        in_specs=[pl.BlockSpec((tile, depth), lambda i: (2 * side + i, 0)), whole, whole],
        out_specs=pl.BlockSpec((tile, 2 * tokens), lambda i: (i, 0)),
        out_shape=jax.ShapeDtypeStruct((near, 2 * tokens), jnp.bfloat16),
        compiler_params=limit(24),
        cost_estimate=brief,
        name="rotate_in",
    )(basis, first, second)


def contract_kernel(place, l0, l1, l2, l3, gathered, kept, send, left, left_sq, right, right_sq):
    depth = l0.shape[1]
    tokens = depth // 2
    quarter = kept.shape[1]

    @pl.when(pl.program_id(0) == 0)
    def _():
        for k, part in enumerate((l0, l1, l2, l3)):
            left[:, k * depth : (k + 1) * depth] = part[...]
            left_sq[:, k * depth : (k + 1) * depth] = squared(part[...])

    for k, (d, far) in enumerate(((0, 0), (2, 0), (0, 1), (2, 1), (1, 0), (3, 0), (1, 1), (3, 1))):
        index = (place[0] + d) % 4 * 2 + (place[1] + far) % 2
        part = gathered[pl.ds(pl.multiple_of(index * tokens, tokens), tokens), :]
        right[pl.ds(k * tokens, tokens), :] = part
        right_sq[pl.ds(k * tokens, tokens), :] = squared(part)

    scale_part = dot(left_sq[...], right_sq[...])
    grad_part = dot(left[...], right[...])
    kept[0] = scale_part[:quarter]
    kept[1] = grad_part[:quarter]
    send[0] = scale_part[quarter:].astype(send.dtype)
    send[1] = grad_part[quarter:].astype(send.dtype)


def contracted(place, lefts, gathered, lo, hi):
    near, depth = lefts[0].shape
    total = gathered.shape[0]
    tile = total // 12
    quarter = near // 2
    out_spec = pl.BlockSpec((2, quarter, tile), lambda i, s: (0, 0, i))
    return pl.pallas_call(
        contract_kernel,
        grid_spec=pltpu.PrefetchScalarGridSpec(
            num_scalar_prefetch=1,
            grid=((hi - lo) // tile,),
            in_specs=[pl.BlockSpec((near, depth), lambda i, s: (0, 0))] * 4
            + [pl.BlockSpec((total, tile), lambda i, s: (0, lo // tile + i))],
            out_specs=[out_spec, out_spec],
            scratch_shapes=[pltpu.VMEM((near, total), jnp.bfloat16)] * 2
            + [pltpu.VMEM((total, tile), jnp.bfloat16)] * 2,
        ),
        out_shape=[
            jax.ShapeDtypeStruct((2, quarter, hi - lo), jnp.float32),
            jax.ShapeDtypeStruct((2, quarter, hi - lo), jnp.bfloat16),
        ],
        compiler_params=limit(53),
        cost_estimate=brief,
        name="contract",
    )(place, *lefts, gathered)


def natural_kernel(left, basis, *refs):
    natural = refs[-1]
    natural[...] = dot(left[...], basis[...], ((1,), (1,))).astype(natural.dtype)


def natural_of(left, basis, natural, b, width):
    quarter, block = left.shape
    tile = 512
    held = [] if natural is None else [natural]
    return pl.pallas_call(
        natural_kernel,
        grid=(block // tile,),
        in_specs=[
            pl.BlockSpec((quarter, block), lambda i: (0, 0)),
            pl.BlockSpec((tile, block), lambda i: (i, 0)),
        ]
        + [pl.BlockSpec(memory_space=pl.ANY)] * len(held),
        out_specs=pl.BlockSpec((quarter, tile), lambda i: (0, b * block // tile + i)),
        out_shape=jax.ShapeDtypeStruct((quarter, width), jnp.bfloat16),
        input_output_aliases={2: 0} if held else {},
        compiler_params=pltpu.CompilerParams(vmem_limit_bytes=24 * 1024 * 1024),
        cost_estimate=brief,
        name="natural",
    )(left, basis, *held)


def shards(activations, out_grads, basis_in, basis_out):
    tokens, half_in = activations.shape
    block = basis_in.shape[1]
    width = out_grads.shape[1]
    quarter = block // 4
    near = block // 2
    x = lax.axis_index("x")
    y = lax.axis_index("y")
    z_lo = lax.axis_index("z_lo")
    core = lax.axis_index("core")
    q = 2 * lax.axis_index("z_hi") + core
    place = jnp.stack([y, core])

    mine = transpose_xy(activations)
    block_basis = lax.dynamic_index_in_dim(basis_in, x, 0, keepdims=False)
    order = [q, q ^ 2, q ^ 1, q ^ 3]
    by_column = jnp.concatenate(
        [lax.dynamic_slice_in_dim(block_basis, k * quarter, quarter, 1) for k in order], 1
    )
    basis_turn = jnp.concatenate(
        [lax.dynamic_slice_in_dim(by_column, k * half_in, half_in, 0) for k in (z_lo, 1 - z_lo)], 0
    ).T
    basis_rows = lax.dynamic_slice_in_dim(by_column, q * quarter, quarter, 0)

    def rotated_out(lo, hi):
        b = lo // block
        return dot(
            out_grads[:, b * block : (b + 1) * block], basis_out[b, :, lo - b * block : hi - b * block]
        ).astype(jnp.bfloat16)

    cut = block * 3 // 2
    first_out = jnp.concatenate([rotated_out(0, block), rotated_out(block, cut)], 1)
    second_out = rotated_out(cut, width)
    mine, basis_turn, basis_rows, second_out = fence(mine, basis_turn, basis_rows, second_out)
    gathered = [lax.all_gather(v, ("x", "core"), axis=0, tiled=True) for v in (first_out, second_out)]

    other = swap(mine, "z_lo")
    two = along_y(mine, 2)
    mine, other, two = fence(mine, other, two)

    whole = jnp.concatenate([mine, other], 1)
    below, above = along_y(whole, 1), along_y(whole, -1)
    two = jnp.concatenate([two, swap(two, "z_lo")], 1)
    send_in = rotated(basis_turn, whole, two, 1)
    early = [rotated(basis_turn, whole, two, 0), swap(send_in, "core")]
    below, above, *early = fence(below, above, *early)

    send_in = rotated(basis_turn, above, below, 1)
    lefts = early + [rotated(basis_turn, above, below, 0), swap(send_in, "core")]

    def finished(own, got):
        total = own + got.astype(jnp.float32)
        tokens_all = tokens * 16
        scales = total[0] / tokens_all
        turned = (total[1] / math.sqrt(tokens_all) / (scales + damping)).astype(jnp.bfloat16)
        return scales, turned

    def from_all_rows(turned, over):
        pair = jnp.concatenate([turned, over], 0)
        total = dot(basis_rows[:, :near], pair) + dot(basis_rows[:, near:], swap(pair, "core"))
        return total.astype(jnp.bfloat16)

    cuts = [0, block // 4, block // 2, block, block * 3 // 2, 2 * block]
    own, out = [], []
    for lo, hi in zip(cuts[:-1], cuts[1:]):
        piece = 0 if hi <= cut else 1
        here = gathered[piece]
        if out:
            here = fence(here, out[-1])[0]
        kept, send = contracted(place, lefts, here, lo - piece * cut, hi - piece * cut)
        own.append(kept)
        out.append(send)
    done = [finished(own[k], swap(out[k], "z_hi")) for k in range(5)]
    turned0 = jnp.concatenate([columns for _, columns in done[:3]], 1)
    left0 = from_all_rows(turned0, swap(turned0, "z_hi"))
    natural = natural_of(left0, basis_out[0], None, 0, width)
    left3 = from_all_rows(done[3][1], swap(done[3][1], "z_hi"))
    scales = jnp.concatenate([scale for scale, _ in done], 1)
    over4, left3, natural, scales = fence(swap(done[4][1], "z_hi"), left3, natural, scales)
    left4 = from_all_rows(done[4][1], over4)
    natural = natural_of(jnp.concatenate([left3, left4], 1), basis_out[1], natural, 1, width)
    return scales, natural


def solution(mesh):
    split = Mesh(mesh.devices.reshape(4, 2, 2, 4, 2), ("x", "z_hi", "core", "y", "z_lo"))
    dp, tensor = ("x", "z_hi", "core"), ("y", "z_lo")
    return jax.shard_map(
        shards,
        mesh=split,
        in_specs=(P(dp, tensor), P(dp, tensor), P(), P(tensor, None, None)),
        out_specs=(P(dp, tensor), P(dp, tensor)),
        check_vma=False,
    )
```

profile of v0, /device:TPU:1, one launch (start us, length us, event | category | flops | bytes accessed | tf_op | source)
XLA Modules:
  0.0 180.5 jit_solution(7634418072193039674)
XLA Ops:
  7.2 2.1 %convolution_convert_fusion.1 = bf16[384,512]{1,0:T(8,128)(2,1)S(1)} fusion(bf16[2,1024,1024]{2,1,0:T(8,128)(2,1)} %param.7, bf16[384,2048]{1,0:T(8,128)(2,1)} %param.5), kind=kOutput, calls=%fused_computation.7 | convolution fusion | flops 402849792 | bytes 2228224 | tf_op jit(solution)/shard_map/dot_general | solution.py:31
  9.4 2.6 %convolution_convert_fusion = bf16[384,1024]{1,0:T(8,128)(2,1)S(1)} fusion(bf16[384,2048]{1,0:T(8,128)(2,1)S(1)} %copy-done.10, bf16[2,1024,1024]{2,1,0:T(8,128)(2,1)} %param.7), kind=kOutput, calls=%fused_computation.4 | convolution fusion | flops 805699584 | bytes 3670016 | tf_op jit(solution)/shard_map/dot_general | solution.py:31
  13.9 2.9 %constant_dynamic-slice_fusion.6 = (bf16[1,1024,256]{2,1,0:T(8,128)(2,1)S(1)}, bf16[1,1024,256]{2,1,0:T(8,128)(2,1)S(1)}, bf16[1,1024,256]{2,1,0:T(8,128)(2,1)S(1)}, bf16[1,1024,256]{2,1,0:T(8,128)(2,1)S(1)}) fusion(bf16[4,1024,1024]{2,1,0:T(8,128)(2,1)} %param.6, s32[]{:T(128)S(6)} %select_n.34, s32[]{:T(128)S(6)} %select_n.36, s32[]{:T(128)S(6)} %select_n.38, ...), kind=kLoop, calls=%fused_computation.85 | loop fusion | bytes 4194324 | tf_op jit(solution)/shard_map/dynamic_slice | solution.py:164
  19.4 2.5 %convolution_convert_fusion.2 = bf16[384,512]{1,0:T(8,128)(2,1)} fusion(bf16[2,1024,1024]{2,1,0:T(8,128)(2,1)} %param.7, bf16[384,2048]{1,0:T(8,128)(2,1)S(1)} %copy-done.11), kind=kOutput, calls=%fused_computation.8 | convolution fusion | flops 402849792 | bytes 2228224 | tf_op jit(solution)/shard_map/dot_general | solution.py:31
  22.0 2.5 %collective-permute-start.1 = (bf16[384,512]{1,0:T(8,128)(2,1)S(1)}, bf16[384,512]{1,0:T(8,128)(2,1)S(1)}, u32[]{:S(2)}, u32[]{:S(2)}) collective-permute-start(bf16[384,512]{1,0:T(8,128)(2,1)S(1)} %collective-permute-done), channel_id=1, source_target_pairs={{0,1},{1,0},{2,3},{3,2},{4,5},{5,4},{6,7},{7,6},{8,9},{9,8},{10,11... | collective-permute-start | bytes 1179656 | tf_op jit(solution)/shard_map/ppermute | solution.py:19
  24.6 14.3 %collective-permute-start.2 = (bf16[384,512]{1,0:T(8,128)(2,1)S(1)}, bf16[384,512]{1,0:T(8,128)(2,1)S(1)}, u32[]{:S(2)}, u32[]{:S(2)}) collective-permute-start(bf16[384,512]{1,0:T(8,128)(2,1)S(1)} %collective-permute-done), channel_id=1, source_target_pairs={{0,4},{2,6},{4,0},{6,2},{1,5},{3,7},{5,1},{7,3},{8,12},{10,14},{12... | collective-permute-start | bytes 1179656 | tf_op jit(solution)/shard_map/ppermute | solution.py:15
  38.9 6.7 %collective-permute-done.2 = bf16[384,512]{1,0:T(8,128)(2,1)S(1)} collective-permute-done((bf16[384,512]{1,0:T(8,128)(2,1)S(1)}, bf16[384,512]{1,0:T(8,128)(2,1)S(1)}, u32[]{:S(2)}, u32[]{:S(2)}) %collective-permute-start.2) | collective-permute-done | bytes 393248 | tf_op jit(solution)/shard_map/ppermute | solution.py:15
  46.1 9.6 %collective-permute-start.3 = (bf16[384,1024]{1,0:T(8,128)(2,1)S(1)}, bf16[384,1024]{1,0:T(8,128)(2,1)S(1)}, u32[]{:S(2)}, u32[]{:S(2)}) collective-permute-start(bf16[384,1024]{1,0:T(8,128)(2,1)S(1)} %constant_dynamic-update-slice_fusion.first), channel_id=1, source_target_pairs={{0,2},{2,4},{4,6},{6,0},{1,3},{3,5},{5,7},{7,1},{8,10},{10,12},{12... | collective-permute-start | bytes 2359304 | tf_op jit(solution)/shard_map/ppermute | solution.py:15
  55.7 2.1 %collective-permute-start.4 = (bf16[384,1024]{1,0:T(8,128)(2,1)S(1)}, bf16[384,1024]{1,0:T(8,128)(2,1)S(1)}, u32[]{:S(2)}, u32[]{:S(2)}) collective-permute-start(bf16[384,1024]{1,0:T(8,128)(2,1)S(1)} %constant_dynamic-update-slice_fusion.first), channel_id=1, source_target_pairs={{0,6},{2,0},{4,2},{6,4},{1,7},{3,1},{5,3},{7,5},{8,14},{10,8},{12,... | collective-permute-start | bytes 2359304 | tf_op jit(solution)/shard_map/ppermute | solution.py:15
  57.9 1.5 rotate_in.5
  59.4 3.7 %collective-permute-start.6 = (bf16[512,768]{1,0:T(8,128)(2,1)S(1)}, bf16[512,768]{1,0:T(8,128)(2,1)S(1)}, u32[]{:S(2)}, u32[]{:S(2)}) collective-permute-start(bf16[512,768]{1,0:T(8,128)(2,1)S(1)} %rotate_in.5), channel_id=1, source_target_pairs={{0,8},{8,0},{1,9},{9,1},{2,10},{10,2},{3,11},{11,3},{4,12},{12,4},... | collective-permute-start | bytes 2359304 | tf_op jit(solution)/shard_map/ppermute | solution.py:19
  63.1 1.4 rotate_in.4.l0
  64.6 7.7 %collective-permute-done.3.second = bf16[384,1024]{1,0:T(8,128)(2,1)S(1)} collective-permute-done((bf16[384,1024]{1,0:T(8,128)(2,1)S(1)}, bf16[384,1024]{1,0:T(8,128)(2,1)S(1)}, u32[]{:S(2)}, u32[]{:S(2)}) %collective-permute-start.3) | collective-permute-done | bytes 786464 | tf_op jit(solution)/shard_map/ppermute | solution.py:15
  72.3 2.2 %rotate_in.7 = bf16[512,768]{1,0:T(8,128)(2,1)} custom-call(bf16[1024,1024]{1,0:T(8,128)(2,1)S(1)} %maximum_bitcast_fusion.basis, bf16[384,1024]{1,0:T(8,128)(2,1)S(1)} %collective-permute-done.4.first, bf16[384,1024]{1,0:T(8,128)(2,1)S(1)} %collective-permute-done.3.second), custom_call_target="tpu_custom_call" | custom-call | flops 1 | bytes 1 | tf_op jit(solution)/shard_map/rotate_in/pallas_call | solution.py:57
  74.5 4.0 %collective-permute-start.7 = (bf16[512,768]{1,0:T(8,128)(2,1)}, bf16[512,768]{1,0:T(8,128)(2,1)}, u32[]{:S(2)}, u32[]{:S(2)}) collective-permute-start(bf16[512,768]{1,0:T(8,128)(2,1)} %rotate_in.7), channel_id=1, source_target_pairs={{0,8},{8,0},{1,9},{9,1},{2,10},{10,2},{3,11},{11,3},{4,12},{12,4},... | collective-permute-start | bytes 2359304 | tf_op jit(solution)/shard_map/ppermute | solution.py:19
  79.7 1.4 rotate_in.6.l2
  82.1 4.7 %contract.5 = (f32[2,256,256]{2,1,0:T(8,128)S(1)}, bf16[2,256,256]{2,1,0:T(8,128)(2,1)S(1)}) custom-call(s32[2]{0:T(128)S(1)} %pad_add_fusion.place, bf16[512,768]{1,0:T(8,128)(2,1)} %copy-done, bf16[512,768]{1,0:T(8,128)(2,1)} %copy-done.4, bf16[512,768]{1,0:T(8,128)(2,1)} %copy-done.1, bf16[512,768]{1,0:T(8,128)(2,1)} %collective-permute-done.7.l3, ...), custom_call_target="tpu_custom_call" | custom-call | flops 1 | bytes 1 | tf_op jit(solution)/shard_map/contract/pallas_call | solution.py:100
  86.8 3.6 %collective-permute-start.13 = (bf16[2,256,256]{2,1,0:T(8,128)(2,1)S(1)}, bf16[2,256,256]{2,1,0:T(8,128)(2,1)}, u32[]{:S(2)}, u32[]{:S(2)}) collective-permute-start(bf16[2,256,256]{2,1,0:T(8,128)(2,1)S(1)} %get-tuple-element.41), channel_id=1, source_target_pairs={{0,16},{16,0},{1,17},{17,1},{2,18},{18,2},{3,19},{19,3},{4,20},{20... | collective-permute-start | bytes 786440 | tf_op jit(solution)/shard_map/ppermute | solution.py:19
  90.4 4.7 %contract.6 = (f32[2,256,256]{2,1,0:T(8,128)S(1)}, bf16[2,256,256]{2,1,0:T(8,128)(2,1)S(1)}) custom-call(s32[2]{0:T(128)S(1)} %pad_add_fusion.place, bf16[512,768]{1,0:T(8,128)(2,1)} %copy-done, bf16[512,768]{1,0:T(8,128)(2,1)} %copy-done.4, bf16[512,768]{1,0:T(8,128)(2,1)} %copy-done.1, bf16[512,768]{1,0:T(8,128)(2,1)} %collective-permute-done.7.l3, ...), custom_call_target="tpu_custom_call" | custom-call | flops 1 | bytes 1 | tf_op jit(solution)/shard_map/contract/pallas_call | solution.py:100
  95.4 7.8 %contract.7 = (f32[2,256,512]{2,1,0:T(8,128)}, bf16[2,256,512]{2,1,0:T(8,128)(2,1)S(1)}) custom-call(s32[2]{0:T(128)S(1)} %pad_add_fusion.place, bf16[512,768]{1,0:T(8,128)(2,1)} %copy-done, bf16[512,768]{1,0:T(8,128)(2,1)} %copy-done.4, bf16[512,768]{1,0:T(8,128)(2,1)} %copy-done.1, bf16[512,768]{1,0:T(8,128)(2,1)} %collective-permute-done.7.l3, ...), custom_call_target="tpu_custom_call" | custom-call | flops 1 | bytes 1 | tf_op jit(solution)/shard_map/contract/pallas_call | solution.py:100
  103.2 2.7 %collective-permute-start.15 = (bf16[2,256,512]{2,1,0:T(8,128)(2,1)S(1)}, bf16[2,256,512]{2,1,0:T(8,128)(2,1)}, u32[]{:S(2)}, u32[]{:S(2)}) collective-permute-start(bf16[2,256,512]{2,1,0:T(8,128)(2,1)S(1)} %get-tuple-element.45), channel_id=1, source_target_pairs={{0,16},{16,0},{1,17},{17,1},{2,18},{18,2},{3,19},{19,3},{4,20},{20... | collective-permute-start | bytes 1572872 | tf_op jit(solution)/shard_map/ppermute | solution.py:19
  106.0 7.7 %contract.8 = (f32[2,256,512]{2,1,0:T(8,128)}, bf16[2,256,512]{2,1,0:T(8,128)(2,1)S(1)}) custom-call(s32[2]{0:T(128)S(1)} %pad_add_fusion.place, bf16[512,768]{1,0:T(8,128)(2,1)} %copy-done, bf16[512,768]{1,0:T(8,128)(2,1)} %copy-done.4, bf16[512,768]{1,0:T(8,128)(2,1)} %copy-done.1, bf16[512,768]{1,0:T(8,128)(2,1)} %collective-permute-done.7.l3, ...), custom_call_target="tpu_custom_call" | custom-call | flops 1 | bytes 1 | tf_op jit(solution)/shard_map/contract/pallas_call | solution.py:100
  113.9 7.7 %contract.9 = (f32[2,256,512]{2,1,0:T(8,128)}, bf16[2,256,512]{2,1,0:T(8,128)(2,1)S(1)}) custom-call(s32[2]{0:T(128)S(1)} %pad_add_fusion.place, bf16[512,768]{1,0:T(8,128)(2,1)} %copy-done, bf16[512,768]{1,0:T(8,128)(2,1)} %copy-done.4, bf16[512,768]{1,0:T(8,128)(2,1)} %copy-done.1, bf16[512,768]{1,0:T(8,128)(2,1)} %collective-permute-done.7.l3, ...), custom_call_target="tpu_custom_call" | custom-call | flops 1 | bytes 1 | tf_op jit(solution)/shard_map/contract/pallas_call | solution.py:100
  121.6 2.7 %collective-permute-start.8 = (bf16[2,256,512]{2,1,0:T(8,128)(2,1)S(1)}, bf16[2,256,512]{2,1,0:T(8,128)(2,1)S(1)}, u32[]{:S(2)}, u32[]{:S(2)}) collective-permute-start(bf16[2,256,512]{2,1,0:T(8,128)(2,1)S(1)} %get-tuple-element.50), channel_id=1, source_target_pairs={{0,16},{16,0},{1,17},{17,1},{2,18},{18,2},{3,19},{19,3},{4,20},{20... | collective-permute-start | bytes 1572872 | tf_op jit(solution)/shard_map/ppermute | solution.py:19
  127.5 1.9 %collective-permute-done.10 = bf16[2,256,512]{2,1,0:T(8,128)(2,1)} collective-permute-done((bf16[2,256,512]{2,1,0:T(8,128)(2,1)S(1)}, bf16[2,256,512]{2,1,0:T(8,128)(2,1)}, u32[]{:S(2)}, u32[]{:S(2)}) %collective-permute-start.10) | collective-permute-done | bytes 524320 | tf_op jit(solution)/shard_map/ppermute | solution.py:19
  130.9 2.4 %collective-permute-start.11 = (bf16[256,512]{1,0:T(8,128)(2,1)S(1)}, bf16[256,512]{1,0:T(8,128)(2,1)S(1)}, u32[]{:S(2)}, u32[]{:S(2)}) collective-permute-start(bf16[256,512]{1,0:T(8,128)(2,1)S(1)} %get-tuple-element.71), channel_id=1, source_target_pairs={{0,16},{16,0},{1,17},{17,1},{2,18},{18,2},{3,19},{19,3},{4,20},{20... | collective-permute-start | bytes 786440 | tf_op jit(solution)/shard_map/ppermute | solution.py:19
  133.8 23.6 %collective-permute-done.11 = bf16[256,512]{1,0:T(8,128)(2,1)S(1)} collective-permute-done((bf16[256,512]{1,0:T(8,128)(2,1)S(1)}, bf16[256,512]{1,0:T(8,128)(2,1)S(1)}, u32[]{:S(2)}, u32[]{:S(2)}) %collective-permute-start.11) | collective-permute-done | bytes 262176 | tf_op jit(solution)/shard_map/ppermute | solution.py:19
  159.1 3.0 %collective-permute-start.9 = (bf16[256,512]{1,0:T(8,128)(2,1)S(1)}, bf16[256,512]{1,0:T(8,128)(2,1)S(1)}, u32[]{:S(2)}, u32[]{:S(2)}) collective-permute-start(bf16[256,512]{1,0:T(8,128)(2,1)S(1)} %get-tuple-element.69), channel_id=1, source_target_pairs={{0,16},{16,0},{1,17},{17,1},{2,18},{18,2},{3,19},{19,3},{4,20},{20... | collective-permute-start | bytes 786440 | tf_op jit(solution)/shard_map/ppermute | solution.py:19
  163.7 1.7 natural.2.refs_0_
  165.4 2.9 %collective-permute-done.9 = bf16[256,512]{1,0:T(8,128)(2,1)S(1)} collective-permute-done((bf16[256,512]{1,0:T(8,128)(2,1)S(1)}, bf16[256,512]{1,0:T(8,128)(2,1)S(1)}, u32[]{:S(2)}, u32[]{:S(2)}) %collective-permute-start.9) | collective-permute-done | bytes 262176 | tf_op jit(solution)/shard_map/ppermute | solution.py:19
  169.7 1.5 collective-permute-done.18
  172.0 1.7 natural.3
  (89 shorter events, 18.0 us)
Async XLA Ops:
  7.2 2.2 %copy-start.10 = (bf16[384,2048]{1,0:T(8,128)(2,1)S(1)}, bf16[384,2048]{1,0:T(8,128)(2,1)}, u32[]{:S(2)}) copy-start(bf16[384,2048]{1,0:T(8,128)(2,1)} %param.5) | copy-start | bytes 4718596
  7.2 74.9 %all-gather.5.cloned.1.call-start = ((), (), s32[]{:S(2)}) async-start(), calls=%async_computation.1 | async-start | bytes 10616832 | tf_op jit(solution)/shard_map/all_gather | solution.py:181
  12.0 1.2 copy-start.12
  13.1 100.8 %all-gather.3.cloned.1.call-start = ((), (), s32[]{:S(2)}) async-start(), calls=%async_computation | async-start | bytes 3538944 | tf_op jit(solution)/shard_map/all_gather | solution.py:181
  13.1 8.8 %collective-permute-start = (bf16[384,512]{1,0:T(8,128)(2,1)S(1)}, bf16[384,512]{1,0:T(8,128)(2,1)S(1)}, u32[]{:S(2)}, u32[]{:S(2)}) collective-permute-start(bf16[384,512]{1,0:T(8,128)(2,1)S(1)} %copy-done.12), channel_id=1, source_target_pairs={{0,0},{2,32},{4,64},{6,96},{32,2},{34,34},{36,66},{38,98},{64,4},{... | collective-permute-start | bytes 1179656 | tf_op jit(solution)/shard_map/ppermute | solution.py:23
  18.0 1.4 copy-start.11
  22.0 16.9 %collective-permute-start.1 = (bf16[384,512]{1,0:T(8,128)(2,1)S(1)}, bf16[384,512]{1,0:T(8,128)(2,1)S(1)}, u32[]{:S(2)}, u32[]{:S(2)}) collective-permute-start(bf16[384,512]{1,0:T(8,128)(2,1)S(1)} %collective-permute-done), channel_id=1, source_target_pairs={{0,1},{1,0},{2,3},{3,2},{4,5},{5,4},{6,7},{7,6},{8,9},{9,8},{10,11... | collective-permute-start | bytes 1179656 | tf_op jit(solution)/shard_map/ppermute | solution.py:19
  24.6 21.0 %collective-permute-start.2 = (bf16[384,512]{1,0:T(8,128)(2,1)S(1)}, bf16[384,512]{1,0:T(8,128)(2,1)S(1)}, u32[]{:S(2)}, u32[]{:S(2)}) collective-permute-start(bf16[384,512]{1,0:T(8,128)(2,1)S(1)} %collective-permute-done), channel_id=1, source_target_pairs={{0,4},{2,6},{4,0},{6,2},{1,5},{3,7},{5,1},{7,3},{8,12},{10,14},{12... | collective-permute-start | bytes 1179656 | tf_op jit(solution)/shard_map/ppermute | solution.py:15
  45.6 12.3 %collective-permute-start.5 = (bf16[384,512]{1,0:T(8,128)(2,1)S(1)}, bf16[384,512]{1,0:T(8,128)(2,1)S(1)}, u32[]{:S(2)}, u32[]{:S(2)}) collective-permute-start(bf16[384,512]{1,0:T(8,128)(2,1)S(1)} %collective-permute-done.2), channel_id=1, source_target_pairs={{0,1},{1,0},{2,3},{3,2},{4,5},{5,4},{6,7},{7,6},{8,9},{9,8},{10,11... | collective-permute-start | bytes 1179656 | tf_op jit(solution)/shard_map/ppermute | solution.py:19
  46.1 26.2 %collective-permute-start.3 = (bf16[384,1024]{1,0:T(8,128)(2,1)S(1)}, bf16[384,1024]{1,0:T(8,128)(2,1)S(1)}, u32[]{:S(2)}, u32[]{:S(2)}) collective-permute-start(bf16[384,1024]{1,0:T(8,128)(2,1)S(1)} %constant_dynamic-update-slice_fusion.first), channel_id=1, source_target_pairs={{0,2},{2,4},{4,6},{6,0},{1,3},{3,5},{5,7},{7,1},{8,10},{10,12},{12... | collective-permute-start | bytes 2359304 | tf_op jit(solution)/shard_map/ppermute | solution.py:15
  55.7 16.6 %collective-permute-start.4 = (bf16[384,1024]{1,0:T(8,128)(2,1)S(1)}, bf16[384,1024]{1,0:T(8,128)(2,1)S(1)}, u32[]{:S(2)}, u32[]{:S(2)}) collective-permute-start(bf16[384,1024]{1,0:T(8,128)(2,1)S(1)} %constant_dynamic-update-slice_fusion.first), channel_id=1, source_target_pairs={{0,6},{2,0},{4,2},{6,4},{1,7},{3,1},{5,3},{7,5},{8,14},{10,8},{12,... | collective-permute-start | bytes 2359304 | tf_op jit(solution)/shard_map/ppermute | solution.py:15
  59.4 12.9 %collective-permute-start.6 = (bf16[512,768]{1,0:T(8,128)(2,1)S(1)}, bf16[512,768]{1,0:T(8,128)(2,1)S(1)}, u32[]{:S(2)}, u32[]{:S(2)}) collective-permute-start(bf16[512,768]{1,0:T(8,128)(2,1)S(1)} %rotate_in.5), channel_id=1, source_target_pairs={{0,8},{8,0},{1,9},{9,1},{2,10},{10,2},{3,11},{11,3},{4,12},{12,4},... | collective-permute-start | bytes 2359304 | tf_op jit(solution)/shard_map/ppermute | solution.py:19
  64.6 10.0 %copy-start = (bf16[512,768]{1,0:T(8,128)(2,1)}, bf16[512,768]{1,0:T(8,128)(2,1)S(1)}, u32[]{:S(2)}) copy-start(bf16[512,768]{1,0:T(8,128)(2,1)S(1)} %rotate_in.4.l0) | copy-start | bytes 2359300
  72.3 2.2 %copy-start.2 = (bf16[384,1024]{1,0:T(8,128)(2,1)}, bf16[384,1024]{1,0:T(8,128)(2,1)S(1)}, u32[]{:S(2)}) copy-start(bf16[384,1024]{1,0:T(8,128)(2,1)S(1)} %collective-permute-done.4.first) | copy-start | bytes 2359300
  72.3 2.2 %copy-start.4 = (bf16[512,768]{1,0:T(8,128)(2,1)}, bf16[512,768]{1,0:T(8,128)(2,1)S(1)}, u32[]{:S(2)}) copy-start(bf16[512,768]{1,0:T(8,128)(2,1)S(1)} %collective-permute-done.6.l1) | copy-start | bytes 2359300
  74.5 7.6 %collective-permute-start.7 = (bf16[512,768]{1,0:T(8,128)(2,1)}, bf16[512,768]{1,0:T(8,128)(2,1)}, u32[]{:S(2)}, u32[]{:S(2)}) collective-permute-start(bf16[512,768]{1,0:T(8,128)(2,1)} %rotate_in.7), channel_id=1, source_target_pairs={{0,8},{8,0},{1,9},{9,1},{2,10},{10,2},{3,11},{11,3},{4,12},{12,4},... | collective-permute-start | bytes 2359304 | tf_op jit(solution)/shard_map/ppermute | solution.py:19
  86.8 37.6 %collective-permute-start.13 = (bf16[2,256,256]{2,1,0:T(8,128)(2,1)S(1)}, bf16[2,256,256]{2,1,0:T(8,128)(2,1)}, u32[]{:S(2)}, u32[]{:S(2)}) collective-permute-start(bf16[2,256,256]{2,1,0:T(8,128)(2,1)S(1)} %get-tuple-element.41), channel_id=1, source_target_pairs={{0,16},{16,0},{1,17},{17,1},{2,18},{18,2},{3,19},{19,3},{4,20},{20... | collective-permute-start | bytes 786440 | tf_op jit(solution)/shard_map/ppermute | solution.py:19
  95.1 30.4 %collective-permute-start.14 = (bf16[2,256,256]{2,1,0:T(8,128)(2,1)S(1)}, bf16[2,256,256]{2,1,0:T(8,128)(2,1)S(1)}, u32[]{:S(2)}, u32[]{:S(2)}) collective-permute-start(bf16[2,256,256]{2,1,0:T(8,128)(2,1)S(1)} %get-tuple-element.43), channel_id=1, source_target_pairs={{0,16},{16,0},{1,17},{17,1},{2,18},{18,2},{3,19},{19,3},{4,20},{20... | collective-permute-start | bytes 786440 | tf_op jit(solution)/shard_map/ppermute | solution.py:19
  103.2 22.5 %collective-permute-start.15 = (bf16[2,256,512]{2,1,0:T(8,128)(2,1)S(1)}, bf16[2,256,512]{2,1,0:T(8,128)(2,1)}, u32[]{:S(2)}, u32[]{:S(2)}) collective-permute-start(bf16[2,256,512]{2,1,0:T(8,128)(2,1)S(1)} %get-tuple-element.45), channel_id=1, source_target_pairs={{0,16},{16,0},{1,17},{17,1},{2,18},{18,2},{3,19},{19,3},{4,20},{20... | collective-permute-start | bytes 1572872 | tf_op jit(solution)/shard_map/ppermute | solution.py:19
  113.7 15.7 %collective-permute-start.10 = (bf16[2,256,512]{2,1,0:T(8,128)(2,1)S(1)}, bf16[2,256,512]{2,1,0:T(8,128)(2,1)}, u32[]{:S(2)}, u32[]{:S(2)}) collective-permute-start(bf16[2,256,512]{2,1,0:T(8,128)(2,1)S(1)} %get-tuple-element.47), channel_id=1, source_target_pairs={{0,16},{16,0},{1,17},{17,1},{2,18},{18,2},{3,19},{19,3},{4,20},{20... | collective-permute-start | bytes 1572872 | tf_op jit(solution)/shard_map/ppermute | solution.py:19
  121.6 37.1 %collective-permute-start.8 = (bf16[2,256,512]{2,1,0:T(8,128)(2,1)S(1)}, bf16[2,256,512]{2,1,0:T(8,128)(2,1)S(1)}, u32[]{:S(2)}, u32[]{:S(2)}) collective-permute-start(bf16[2,256,512]{2,1,0:T(8,128)(2,1)S(1)} %get-tuple-element.50), channel_id=1, source_target_pairs={{0,16},{16,0},{1,17},{17,1},{2,18},{18,2},{3,19},{19,3},{4,20},{20... | collective-permute-start | bytes 1572872 | tf_op jit(solution)/shard_map/ppermute | solution.py:19
  124.4 1.3 copy-start.8
  126.9 2.5 %copy-start.7 = (f32[2,256,512]{2,1,0:T(8,128)S(1)}, f32[2,256,512]{2,1,0:T(8,128)}, u32[]{:S(2)}) copy-start(f32[2,256,512]{2,1,0:T(8,128)} %get-tuple-element.52) | copy-start | bytes 3145732
  127.2 31.4 %collective-permute-start.16 = (bf16[256,1024]{1,0:T(8,128)(2,1)S(1)}, bf16[256,1024]{1,0:T(8,128)(2,1)S(1)}, u32[]{:S(2)}, u32[]{:S(2)}) collective-permute-start(bf16[256,1024]{1,0:T(8,128)(2,1)S(1)} %pad_maximum_fusion.4), channel_id=1, source_target_pairs={{0,16},{16,0},{1,17},{17,1},{2,18},{18,2},{3,19},{19,3},{4,20},{20... | collective-permute-start | bytes 1572872 | tf_op jit(solution)/shard_map/ppermute | solution.py:19
  129.4 3.9 %copy-start.5 = (bf16[2,1024,1024]{2,1,0:T(8,128)(2,1)S(1)}, bf16[2,1024,1024]{2,1,0:T(8,128)(2,1)}, u32[]{:S(2)}) copy-start(bf16[2,1024,1024]{2,1,0:T(8,128)(2,1)} %param.7) | copy-start | bytes 12582916
  130.9 26.5 %collective-permute-start.11 = (bf16[256,512]{1,0:T(8,128)(2,1)S(1)}, bf16[256,512]{1,0:T(8,128)(2,1)S(1)}, u32[]{:S(2)}, u32[]{:S(2)}) collective-permute-start(bf16[256,512]{1,0:T(8,128)(2,1)S(1)} %get-tuple-element.71), channel_id=1, source_target_pairs={{0,16},{16,0},{1,17},{17,1},{2,18},{18,2},{3,19},{19,3},{4,20},{20... | collective-permute-start | bytes 786440 | tf_op jit(solution)/shard_map/ppermute | solution.py:19
  133.8 25.0 %copy-start.6 = (f32[2,256,512]{2,1,0:T(8,128)S(1)}, f32[2,256,512]{2,1,0:T(8,128)}, u32[]{:S(2)}) copy-start(f32[2,256,512]{2,1,0:T(8,128)} %get-tuple-element.49) | copy-start | bytes 3145732
  157.4 4.7 %collective-permute-start.12 = (bf16[512,512]{1,0:T(8,128)(2,1)S(1)}, bf16[512,512]{1,0:T(8,128)(2,1)S(1)}, u32[]{:S(2)}, u32[]{:S(2)}) collective-permute-start(bf16[512,512]{1,0:T(8,128)(2,1)S(1)} %pad_maximum_fusion.3), channel_id=1, source_target_pairs={{0,8},{8,0},{1,9},{9,1},{2,10},{10,2},{3,11},{11,3},{4,12},{12,4},... | collective-permute-start | bytes 1572872 | tf_op jit(solution)/shard_map/ppermute | solution.py:19
  158.6 4.1 %collective-permute-start.17 = (bf16[512,1024]{1,0:T(8,128)(2,1)S(1)}, bf16[512,1024]{1,0:T(8,128)(2,1)S(1)}, u32[]{:S(2)}, u32[]{:S(2)}) collective-permute-start(bf16[512,1024]{1,0:T(8,128)(2,1)S(1)} %pad_maximum_fusion.2), channel_id=1, source_target_pairs={{0,8},{8,0},{1,9},{9,1},{2,10},{10,2},{3,11},{11,3},{4,12},{12,4},... | collective-permute-start | bytes 3145736 | tf_op jit(solution)/shard_map/ppermute | solution.py:19
  159.1 4.2 %copy-start.9 = (f32[256,2048]{1,0:T(8,128)}, f32[256,2048]{1,0:T(8,128)S(1)}, u32[]{:S(2)}) copy-start(f32[256,2048]{1,0:T(8,128)S(1)} %get-tuple-element.29) | copy-start | bytes 6291460
  159.1 9.2 %collective-permute-start.9 = (bf16[256,512]{1,0:T(8,128)(2,1)S(1)}, bf16[256,512]{1,0:T(8,128)(2,1)S(1)}, u32[]{:S(2)}, u32[]{:S(2)}) collective-permute-start(bf16[256,512]{1,0:T(8,128)(2,1)S(1)} %get-tuple-element.69), channel_id=1, source_target_pairs={{0,16},{16,0},{1,17},{17,1},{2,18},{18,2},{3,19},{19,3},{4,20},{20... | collective-permute-start | bytes 786440 | tf_op jit(solution)/shard_map/ppermute | solution.py:19
  168.3 2.9 %collective-permute-start.18 = (bf16[512,512]{1,0:T(8,128)(2,1)S(1)}, bf16[512,512]{1,0:T(8,128)(2,1)S(1)}, u32[]{:S(2)}, u32[]{:S(2)}) collective-permute-start(bf16[512,512]{1,0:T(8,128)(2,1)S(1)} %pad_maximum_fusion.5), channel_id=1, source_target_pairs={{0,8},{8,0},{1,9},{9,1},{2,10},{10,2},{3,11},{11,3},{4,12},{12,4},... | collective-permute-start | bytes 1572872 | tf_op jit(solution)/shard_map/ppermute | solution.py:19
  (2 other events, 2.0 us)
Sparse Core Ops, SparseCore 0:
  13.2 65.8 all-gather.4
  80.8 27.4 all-gather.2
where the time goes:
time: 181 us
  starting transfers between devices  55.5 us (31%)
  waiting for transfers between devices  44.4 us (25%)
  Pallas kernels  42.6 us (24%)
  between operations  14.6 us (8%)
  matrix products  9.43 us (5%)
  local copies, waits for them, and re-layouts  7.77 us (4%)
  other arithmetic  6.27 us (3%)
    pallas_call x5, Pallas kernels, contracted(): pl.pallas_call(contract_kernel, grid_spec=pltpu.PrefetchScalarGridSpec(nu...  32.6 us
    ppermute x15, waiting for transfers between devices, swap(): return lax.ppermute(v, axis, [(0, 1), (1, 0)])  30 us
    ppermute x15, starting transfers between devices, swap(): return lax.ppermute(v, axis, [(0, 1), (1, 0)])  28.7 us
    ppermute x3, starting transfers between devices, along_y(): return lax.ppermute(v, 'y', [(i, (i + d) % 4) for i in range(4)])  26.1 us
    ppermute x3, waiting for transfers between devices, along_y(): return lax.ppermute(v, 'y', [(i, (i + d) % 4) for i in range(4)])  14.4 us
    dot_general x9, matrix products, dot(): lax.dot_general(left, right, (contract, ((), ())), preferred_element_type...  9.43 us
    pallas_call x4, Pallas kernels, rotated(): pl.pallas_call(rotate_kernel, grid=(2,), in_specs=[pl.BlockSpec((tile, de...  6.56 us
    add x5, other arithmetic, finished(): total = own + got.astype(jnp.float32)  3.88 us
  transfers between devices with their start and end apart: 21, of which 6 were waited for; matrix products, arithmetic and copies ran while one was open for 8% of the time, Pallas kernels for 23%

commit v1 on v0

v1 whole, which is shorter than its diff:
```python
import math

import jax
import jax.numpy as jnp
from jax import lax
from jax.experimental import pallas as pl
from jax.experimental.pallas import tpu as pltpu
from jax.sharding import Mesh
from jax.sharding import PartitionSpec as P

damping = 0.1


def along_y(v, d):
    return lax.ppermute(v, "y", [(i, (i + d) % 4) for i in range(4)])


def along_x(v, d):
    return lax.ppermute(v, "x", [(i, (i + d) % 4) for i in range(4)])


def swap(v, axis):
    return lax.ppermute(v, axis, [(0, 1), (1, 0)])


def transpose_xy(v):
    return lax.ppermute(v, ("x", "y"), [(x * 4 + y, y * 4 + x) for x in range(4) for y in range(4)])


def squared(values):
    return values * values


def dot(left, right, contract=((1,), (0,))):
    return lax.dot_general(left, right, (contract, ((), ())), preferred_element_type=jnp.float32)


def fence(*values):
    return lax.optimization_barrier(values)


brief = pl.CostEstimate(flops=1, bytes_accessed=1, transcendentals=0)


def limit(mib):
    return pltpu.CompilerParams(vmem_limit_bytes=mib * 1024 * 1024)


def pick_kernel(place, values, out):
    out[...] = values[...]


def partner_columns(place, values, block):
    rows = values.shape[0]
    return pl.pallas_call(
        pick_kernel,
        grid_spec=pltpu.PrefetchScalarGridSpec(
            num_scalar_prefetch=1,
            grid=(2,),
            in_specs=[pl.BlockSpec((rows, block // 2), lambda i, s: (0, (1 - s[0]) * 2 + i))],
            out_specs=pl.BlockSpec((rows, block // 2), lambda i, s: (0, i)),
        ),
        out_shape=jax.ShapeDtypeStruct((rows, block), values.dtype),
        compiler_params=limit(60),
        cost_estimate=brief,
        name="partner_columns",
    )(place, values)


def rotate_out_kernel(place, own, other, basis, *outs):
    tokens = own.shape[0]
    for k, out in enumerate(outs):

        @pl.when(pl.program_id(0) == k)
        def _(out=out):
            out[:tokens] = dot(own[...], basis[0]).astype(out.dtype)
            out[tokens:] = dot(other[...], basis[0]).astype(out.dtype)


def rotated_out(place, grads, other, basis):
    tokens, block = other.shape
    tile = block // 4
    shape = jax.ShapeDtypeStruct((2 * tokens, tile), jnp.bfloat16)
    return pl.pallas_call(
        rotate_out_kernel,
        grid_spec=pltpu.PrefetchScalarGridSpec(
            num_scalar_prefetch=1,
            grid=(4,),
            in_specs=[
                pl.BlockSpec((tokens, block), lambda i, s: (0, s[0])),
                pl.BlockSpec((tokens, block), lambda i, s: (0, 0)),
                pl.BlockSpec((1, block, tile), lambda i, s: (s[0], 0, i)),
            ],
            out_specs=[pl.BlockSpec(shape.shape, lambda i, s: (0, 0))] * 4,
        ),
        out_shape=[shape] * 4,
        compiler_params=limit(48),
        cost_estimate=brief,
        name="rotate_out",
    )(place, grads, other, basis)


def payload_kernel(below, above, *refs):
    *own, right, left = refs
    start = 0
    for values in own:
        start = values.shape[1]
        right[:, :start] = values[...]
        left[:, :start] = values[...]
    right[:, start:] = below[...]
    left[:, start:] = above[...]


def payloads(own, columns, below, above, mib=24):
    own = [] if own is None else [own]
    rows = below.shape[0]
    half = columns // 2
    shape = jax.ShapeDtypeStruct((rows, sum(v.shape[1] for v in own) + half), jnp.bfloat16)
    whole = pl.BlockSpec(shape.shape, lambda i: (0, 0))
    return pl.pallas_call(
        payload_kernel,
        grid=(1,),
        in_specs=[pl.BlockSpec((rows, half), lambda i: (0, 0)), pl.BlockSpec((rows, half), lambda i: (0, 1))]
        + [pl.BlockSpec(v.shape, lambda i: (0, 0)) for v in own],
        out_specs=[whole, whole],
        out_shape=[shape, shape],
        compiler_params=limit(mib),
        cost_estimate=brief,
        name="payload",
    )(below, above, *own)


def rotate_kernel(basis, first, second, out):
    tokens = first.shape[0]
    ways = ((1,), (1,))
    out[:, :tokens] = dot(basis[...], first[...], ways).astype(out.dtype)
    out[:, tokens:] = dot(basis[...], second[...], ways).astype(out.dtype)


def rotated(basis, first, second):
    tokens, depth = first.shape
    features = basis.shape[0]
    tile = features // 4
    whole = pl.BlockSpec((tokens, depth), lambda i: (0, 0))
    return pl.pallas_call(
        rotate_kernel,
        grid=(4,),
        in_specs=[pl.BlockSpec((tile, depth), lambda i: (i, 0)), whole, whole],
        out_specs=pl.BlockSpec((tile, 2 * tokens), lambda i: (i, 0)),
        out_shape=jax.ShapeDtypeStruct((features, 2 * tokens), jnp.bfloat16),
        compiler_params=limit(24),
        cost_estimate=brief,
        name="rotate_in",
    )(basis, first, second)


def contract_kernel(place, early, early_far, late, late_far, own, above, below, right, left, *refs):
    kept, send, features, grads, feature_sems, grad_sems = refs
    tokens = features.shape[2] // 2
    columns = grads.shape[2]
    half = columns // 2
    rows = kept.shape[1]

    def feature_copies(e, index, sources):
        for far, source in enumerate(sources):
            start = pl.multiple_of(index // 2 * tokens, tokens)
            yield pltpu.make_async_copy(
                source.at[:, pl.ds(start, tokens)],
                features.at[e, :, pl.ds(far * tokens, tokens)],
                feature_sems.at[e, far],
            )

    def grad_copies(e):
        if e == 2:
            start = right.shape[1] - half
            pairs = [(right.at[:, pl.ds(start, half)], 0), (left.at[:, pl.ds(start, half)], half)]
        else:
            source = {0: own, 1: above, 3: below}[e]
            pairs = [(source.at[:, pl.ds(k * half, half)], k * half) for k in range(2)]
        for k, (source, start) in enumerate(pairs):
            yield pltpu.make_async_copy(source, grads.at[e, :, pl.ds(start, half)], grad_sems.at[e, k])

    for e in range(4):
        index = (place[0] + e) % 4
        for copy in grad_copies(e):
            copy.start()
        for odd, sources in enumerate(((early, early_far), (late, late_far))):

            @pl.when(index % 2 == odd)
            def _(e=e, index=index, sources=sources):
                for copy in feature_copies(e, index, sources):
                    copy.start()

    scale_part, grad_part = None, None
    for e in range(4):
        for copy in grad_copies(e):
            copy.wait()
        for copy in feature_copies(e, 0, (early, early_far)):
            copy.wait()
        part, values = features[e], grads[e]
        grad = dot(part, values)
        scale = dot(squared(part), squared(values))
        grad_part = grad if e == 0 else grad_part + grad
        scale_part = scale if e == 0 else scale_part + scale
    kept[0] = scale_part[:rows]
    kept[1] = grad_part[:rows]
    send[0] = scale_part[rows:].astype(send.dtype)
    send[1] = grad_part[rows:].astype(send.dtype)


def contracted(place, lefts, own, brought, following):
    features, depth = lefts[0].shape
    tokens, columns = own.shape
    rows = features // 2
    out_spec = pl.BlockSpec((2, rows, columns), lambda i, s: (0, 0, 0))
    return pl.pallas_call(
        contract_kernel,
        grid_spec=pltpu.PrefetchScalarGridSpec(
            num_scalar_prefetch=1,
            grid=(1,),
            in_specs=[pl.BlockSpec(memory_space=pl.ANY)] * 9,
            out_specs=[out_spec, out_spec],
            scratch_shapes=[
                pltpu.VMEM((4, features, depth), jnp.bfloat16),
                pltpu.VMEM((4, tokens, columns), jnp.bfloat16),
                pltpu.SemaphoreType.DMA((4, 2)),
                pltpu.SemaphoreType.DMA((4, 2)),
            ],
        ),
        out_shape=[
            jax.ShapeDtypeStruct((2, rows, columns), jnp.float32),
            jax.ShapeDtypeStruct((2, rows, columns), jnp.bfloat16),
        ],
        compiler_params=limit(56),
        cost_estimate=brief,
        name="contract",
    )(place, *lefts, own, brought[1], brought[0], *following)


def natural_kernel(place, left, basis, natural):
    natural[...] = dot(left[...], basis[0], ((1,), (1,))).astype(natural.dtype)


def natural_rows(place, left, basis, whose):
    rows, block = left.shape
    tile = block // 2
    return pl.pallas_call(
        natural_kernel,
        grid_spec=pltpu.PrefetchScalarGridSpec(
            num_scalar_prefetch=1,
            grid=(2,),
            in_specs=[
                pl.BlockSpec((rows // 2, block), lambda i, s: (s[0] ^ whose, 0)),
                pl.BlockSpec((1, tile, block), lambda i, s: (s[0], i, 0)),
            ],
            out_specs=pl.BlockSpec((rows // 2, tile), lambda i, s: (0, i)),
        ),
        out_shape=jax.ShapeDtypeStruct((rows // 2, block), jnp.bfloat16),
        compiler_params=limit(24),
        cost_estimate=brief,
        name="natural",
    )(place, left, basis)


def place_kernel(place, own, other, out):
    @pl.when(pl.program_id(0) == place[0])
    def _():
        out[...] = own[...]

    @pl.when(pl.program_id(0) != place[0])
    def _():
        out[...] = other[...]


def side_by_side(place, own, other):
    rows, block = own.shape
    whole = pl.BlockSpec((rows, block), lambda i, s: (0, 0))
    return pl.pallas_call(
        place_kernel,
        grid_spec=pltpu.PrefetchScalarGridSpec(
            num_scalar_prefetch=1,
            grid=(2,),
            in_specs=[whole, whole],
            out_specs=pl.BlockSpec((rows, block), lambda i, s: (0, i)),
        ),
        out_shape=jax.ShapeDtypeStruct((rows, 2 * block), own.dtype),
        compiler_params=limit(24),
        cost_estimate=brief,
        name="side_by_side",
    )(place, own, other)


def shards(activations, out_grads, basis_in, basis_out):
    tokens, half_in = activations.shape
    block = basis_in.shape[1]
    near = block // 2
    x = lax.axis_index("x")
    y = lax.axis_index("y")
    z_lo = lax.axis_index("z_lo")
    z_hi = lax.axis_index("z_hi")
    core = lax.axis_index("core")
    turn = jnp.reshape((x - y) % 4, (1,))
    place = jnp.reshape(core, (1,))

    mine = transpose_xy(activations)
    other_out = swap(partner_columns(place, out_grads, block), "core")
    block_basis = lax.dynamic_index_in_dim(basis_in, x, 0, keepdims=False)
    by_column = jnp.concatenate(
        [lax.dynamic_slice_in_dim(block_basis, k * near, near, 1) for k in (z_hi, 1 - z_hi)], 1
    )
    basis_turn = jnp.concatenate(
        [lax.dynamic_slice_in_dim(by_column, k * half_in, half_in, 0) for k in (z_lo, 1 - z_lo)], 0
    ).T
    basis_rows = lax.dynamic_slice_in_dim(by_column, z_hi * near, near, 0)
    own_out = rotated_out(place, out_grads, other_out, basis_out)

    def around_x(right, left):
        return [along_x(right, 1), along_x(left, -1)]

    mine, basis_turn, basis_rows, *own_out = fence(mine, basis_turn, basis_rows, *own_out)
    columns = own_out[0].shape[1]

    other = swap(mine, "z_lo")
    two = along_y(mine, 2)
    first = around_x(own_out[0], own_out[0])
    mine, other, two, *first = fence(mine, other, two, *first)

    whole = jnp.concatenate([mine, other], 1)
    sent = payloads(own_out[1], columns, *first)
    whole, two, *sent = fence(whole, two, *sent)
    below, above = along_y(whole, 1), along_y(whole, -1)
    second = around_x(*sent)
    two = jnp.concatenate([two, swap(two, "z_lo")], 1)
    early = rotated(basis_turn, whole, two)
    below, above, early, *second = fence(below, above, early, *second)

    def finished(kept, got):
        total = kept + got.astype(jnp.float32)
        tokens_all = tokens * 16
        scales = total[0] / tokens_all
        turned = (total[1] / math.sqrt(tokens_all) / (scales + damping)).astype(jnp.bfloat16)
        return scales, turned

    def product(turned, over):
        total = dot(basis_rows[:, :near], turned) + dot(basis_rows[:, near:], over)
        return total.astype(jnp.bfloat16)

    third = around_x(*payloads(own_out[2], columns, *second))
    late = rotated(basis_turn, above, below)
    lefts = [early, swap(early, "core"), late, swap(late, "core")]
    kept0, send0 = contracted(turn, lefts, own_out[0], first, second)
    got0 = swap(send0, "z_hi")
    *third, send0 = fence(*third, send0)
    fourth = around_x(*payloads(own_out[3], columns, *third))
    own1, got0 = fence(own_out[1], got0)
    kept1, send1 = contracted(turn, lefts, own1, second, third)
    got1 = swap(send1, "z_hi")
    scales0, turned0 = finished(kept0, got0)
    *fourth, send1, over0 = fence(*fourth, send1, swap(turned0, "z_hi"))
    fifth = around_x(*payloads(None, columns, *fourth, mib=60))
    kept2, send2 = contracted(turn, lefts, own_out[2], third, fourth)
    got2 = swap(send2, "z_hi")
    *fifth, send2, got1 = fence(*fifth, send2, got1)
    kept3, send3 = contracted(turn, lefts, own_out[3], fourth, fifth)

    got3 = swap(send3, "z_hi")
    got1, _ = fence(got1, send3)
    done = [(scales0, turned0)] + [finished(*pair) for pair in ((kept1, got1), (kept2, got2), (kept3, got3))]
    left01 = product(turned0, over0)
    left12 = product(done[1][1], swap(done[1][1], "z_hi"))
    left2 = product(done[2][1], swap(done[2][1], "z_hi"))
    over3 = swap(done[3][1], "z_hi")
    scales = jnp.concatenate([scale for scale, _ in done], 1)
    quarter = near // 2
    scales_own = lax.dynamic_slice_in_dim(scales, core * quarter, quarter, 0)
    scales_other = swap(lax.dynamic_slice_in_dim(scales, (1 - core) * quarter, quarter, 0), "core")
    scales = side_by_side(place, scales_own, scales_other)
    over3, left2, left12, left01, scales = fence(over3, left2, left12, left01, scales)
    left = jnp.concatenate([left01, left12, left2, product(done[3][1], over3)], 1)
    natural_other = swap(natural_rows(place, left, basis_out, 1), "core")
    natural = side_by_side(place, natural_rows(place, left, basis_out, 0), natural_other)
    return scales, natural


def solution(mesh):
    split = Mesh(mesh.devices.reshape(4, 2, 2, 4, 2), ("x", "z_hi", "core", "y", "z_lo"))
    dp, tensor = ("x", "z_hi", "core"), ("y", "z_lo")
    return jax.shard_map(
        shards,
        mesh=split,
        in_specs=(P(dp, tensor), P(dp, tensor), P(), P(tensor, None, None)),
        out_specs=(P(dp, tensor), P(dp, tensor)),
        check_vma=False,
    )
```

time: 181 us -> 175 us (0.967)
  between operations: 14.6 us -> 1.18 us
  Pallas kernels: 42.6 us -> 49.2 us
  matrix products: 9.43 us -> 4.63 us
  starting transfers between devices: 55.5 us -> 57.6 us
  local copies, waits for them, and re-layouts: 7.77 us -> 9.74 us
    ppermute x3, starting transfers between devices: 26.1 us -> 8.45 us  [along_y(): return lax.ppermute(v, 'y', [(i, (i + d) % 4) for i in range(4)])]
    ppermute x0 -> x10, starting transfers between devices: none -> 13.5 us  [along_x(): return lax.ppermute(v, 'x', [(i, (i + d) % 4) for i in range(4)])]
    pallas_call x6 -> x12, Pallas kernels: 9.96 us -> 20.4 us  [the longest x2 5.81 us: rotated(): pl.pallas_call(rotate_kernel, grid=(4,), in_specs=[pl.BlockSpec((tile, de...]
    ppermute x3, waiting for transfers between devices: 14.4 us -> 7.87 us  [along_y(): return lax.ppermute(v, 'y', [(i, (i + d) % 4) for i in range(4)])]
    ppermute x0 -> x10, waiting for transfers between devices: none -> 5.86 us  [along_x(): return lax.ppermute(v, 'x', [(i, (i + d) % 4) for i in range(4)])]
    dot_general x9 -> x8, matrix products: 9.43 us -> 4.63 us  [dot(): lax.dot_general(left, right, (contract, ((), ())), preferred_element_type...]
    pallas_call x5 -> x4, Pallas kernels: 32.6 us -> 28.8 us  [contracted(): pl.pallas_call(contract_kernel, grid_spec=pltpu.PrefetchScalarGridSpec(nu...]
    ppermute x1, starting transfers between devices: 0.69 us -> 4.48 us  [transpose_xy(): lax.ppermute(v, ('x', 'y'), [(x * 4 + y, y * 4 + x) for x in range(4) for...]
  transfers between devices with their start and end apart: 21 -> 29, of which waited for: 6 -> 14; matrix products, arithmetic and copies ran while one was open for 8% -> 9% of each run, Pallas kernels for 23% -> 24%
where the time goes in v1:
time: 175 us; the launch traced here: 174 us
  starting transfers between devices  57.6 us (33%)
  Pallas kernels  49.2 us (28%)
  waiting for transfers between devices  44.3 us (25%)
  local copies, waits for them, and re-layouts  9.74 us (6%)
  other arithmetic  7.51 us (4%)
  matrix products  4.63 us (3%)
    ppermute x15, starting transfers between devices, swap(): return lax.ppermute(v, axis, [(0, 1), (1, 0)])  31.2 us
    ppermute x15, waiting for transfers between devices, swap(): return lax.ppermute(v, axis, [(0, 1), (1, 0)])  30.6 us
    pallas_call x4, Pallas kernels, contracted(): pl.pallas_call(contract_kernel, grid_spec=pltpu.PrefetchScalarGridSpec(nu...  28.8 us
    ppermute x10, starting transfers between devices, along_x(): return lax.ppermute(v, 'x', [(i, (i + d) % 4) for i in range(4)])  13.5 us
    ppermute x3, starting transfers between devices, along_y(): return lax.ppermute(v, 'y', [(i, (i + d) % 4) for i in range(4)])  8.45 us
    ppermute x3, waiting for transfers between devices, along_y(): return lax.ppermute(v, 'y', [(i, (i + d) % 4) for i in range(4)])  7.87 us
    ppermute x10, waiting for transfers between devices, along_x(): return lax.ppermute(v, 'x', [(i, (i + d) % 4) for i in range(4)])  5.86 us
    pallas_call x2, Pallas kernels, rotated(): pl.pallas_call(rotate_kernel, grid=(4,), in_specs=[pl.BlockSpec((tile, de...  5.81 us
  transfers between devices with their start and end apart: 29, of which 14 were waited for; matrix products, arithmetic and copies ran while one was open for 9% of the time, Pallas kernels for 24%

profile of v1, /device:TPU:1, one launch (start us, length us, event | category | flops | bytes accessed | tf_op | source)
XLA Modules:
  0.0 174.2 jit_solution(7104719976510176723)
XLA Ops:
  0.6 2.0 %partner_columns.1 = bf16[384,1024]{1,0:T(8,128)(2,1)} custom-call(s32[1]{0:T(128)} %bitcast.4.place, bf16[384,2048]{1,0:T(8,128)(2,1)} %own.1), custom_call_target="tpu_custom_call" | custom-call | flops 1 | bytes 1 | tf_op jit(solution)/shard_map/partner_columns/pallas_call | solution.py:55
  4.0 4.5 %collective-permute-start = (bf16[384,512]{1,0:T(8,128)(2,1)}, bf16[384,512]{1,0:T(8,128)(2,1)}, u32[]{:S(2)}, u32[]{:S(2)}) collective-permute-start(bf16[384,512]{1,0:T(8,128)(2,1)} %param.4), channel_id=1, source_target_pairs={{0,0},{2,32},{4,64},{6,96},{32,2},{34,34},{36,66},{38,98},{64,4},{... | collective-permute-start | bytes 1179656 | tf_op jit(solution)/shard_map/ppermute | solution.py:27
  8.5 2.7 %constant_dynamic-slice_fusion.2 = (bf16[1,1024,512]{2,1,0:T(8,128)(2,1)S(1)}, bf16[1,1024,512]{2,1,0:T(8,128)(2,1)S(1)}) fusion(bf16[4,1024,1024]{2,1,0:T(8,128)(2,1)} %param.6, s32[]{:T(128)S(6)} %select_n.38, s32[]{:T(128)S(6)} %select_n.42, s32[]{:T(128)S(6)} %select_n.40), kind=kLoop, calls=%fused_computation.64 | loop fusion | bytes 4194316 | tf_op jit(solution)/shard_map/dynamic_slice | solution.py:309
  13.8 2.6 %fusion.4 = (bf16[512,1024]{0,1:T(8,128)(2,1)}, bf16[512,1024]{0,1:T(8,128)(2,1)S(1)}, bf16[512,1024]{0,1:T(8,128)(2,1)S(1)}) fusion(s32[]{:T(128)S(6)} %select_n.39, bf16[1024,512]{0,1:T(8,128)(2,1)} %bitcast.55, bf16[1024,512]{0,1:T(8,128)(2,1)S(1)} %bitcast.54, s32[]{:T(128)S(6)} %select_n.43, s32[]{:T(128)S(6)} %select_n.44), kind=kLoop, calls=%fused_computation.16 | loop fusion | flops 6291456 | bytes 5242892 | tf_op jit(solution)/shard_map/concatenate | solution.py:308
  17.9 3.9 %rotate_out.1 = (bf16[768,256]{1,0:T(8,128)(2,1)S(1)}, bf16[768,256]{1,0:T(8,128)(2,1)S(1)}, bf16[768,256]{1,0:T(8,128)(2,1)S(1)}, bf16[768,256]{1,0:T(8,128)(2,1)S(1)}) custom-call(s32[1]{0:T(128)} %bitcast.4.place, bf16[384,2048]{1,0:T(8,128)(2,1)S(1)} %copy-done.3, bf16[384,1024]{1,0:T(8,128)(2,1)S(1)} %collective-permute-done.1.other, ...), custom_call_target="tpu_custom_call" | custom-call | flops 1 | bytes 1 | tf_op jit(solution)/shard_map/rotate_out/pallas_call | solution.py:84
  21.9 6.9 %collective-permute-start.3 = (bf16[384,512]{1,0:T(8,128)(2,1)}, bf16[384,512]{1,0:T(8,128)(2,1)S(1)}, u32[]{:S(2)}, u32[]{:S(2)}) collective-permute-start(bf16[384,512]{1,0:T(8,128)(2,1)} %collective-permute-done), channel_id=1, source_target_pairs={{0,4},{2,6},{4,0},{6,2},{1,5},{3,7},{5,1},{7,3},{8,12},{10,14},{12... | collective-permute-start | bytes 1179656 | tf_op jit(solution)/shard_map/ppermute | solution.py:15
  30.4 2.7 %collective-permute-start.5 = (bf16[768,256]{1,0:T(8,128)(2,1)S(1)}, bf16[768,256]{1,0:T(8,128)(2,1)S(1)}, u32[]{:S(2)}, u32[]{:S(2)}) collective-permute-start(bf16[768,256]{1,0:T(8,128)(2,1)S(1)} %get-tuple-element.64.own), channel_id=1, source_target_pairs={{0,96},{32,0},{64,32},{96,64},{1,97},{33,1},{65,33},{97,65},{2,98}... | collective-permute-start | bytes 1179656 | tf_op jit(solution)/shard_map/ppermute | solution.py:19
  33.1 4.1 %collective-permute-done.3 = bf16[384,512]{1,0:T(8,128)(2,1)S(1)} collective-permute-done((bf16[384,512]{1,0:T(8,128)(2,1)}, bf16[384,512]{1,0:T(8,128)(2,1)S(1)}, u32[]{:S(2)}, u32[]{:S(2)}) %collective-permute-start.3) | collective-permute-done | bytes 393248 | tf_op jit(solution)/shard_map/ppermute | solution.py:15
  39.9 3.1 %collective-permute-done.4.below = bf16[768,256]{1,0:T(8,128)(2,1)S(1)} collective-permute-done((bf16[768,256]{1,0:T(8,128)(2,1)S(1)}, bf16[768,256]{1,0:T(8,128)(2,1)S(1)}, u32[]{:S(2)}, u32[]{:S(2)}) %collective-permute-start.4) | collective-permute-done | bytes 393248 | tf_op jit(solution)/shard_map/ppermute | solution.py:19
  46.0 2.7 %collective-permute-start.10 = (bf16[768,384]{1,0:T(8,128)(2,1)S(1)}, bf16[768,384]{1,0:T(8,128)(2,1)S(1)}, u32[]{:S(2)}, u32[]{:S(2)}) collective-permute-start(bf16[768,384]{1,0:T(8,128)(2,1)S(1)} %get-tuple-element.77), channel_id=1, source_target_pairs={{0,96},{32,0},{64,32},{96,64},{1,97},{33,1},{65,33},{97,65},{2,98}... | collective-permute-start | bytes 1769480 | tf_op jit(solution)/shard_map/ppermute | solution.py:19
  49.1 6.5 %collective-permute-done.8 = bf16[384,512]{1,0:T(8,128)(2,1)S(1)} collective-permute-done((bf16[384,512]{1,0:T(8,128)(2,1)S(1)}, bf16[384,512]{1,0:T(8,128)(2,1)S(1)}, u32[]{:S(2)}, u32[]{:S(2)}) %collective-permute-start.8) | collective-permute-done | bytes 393248 | tf_op jit(solution)/shard_map/ppermute | solution.py:23
  55.7 2.9 %rotate_in.2.early = bf16[1024,768]{1,0:T(8,128)(2,1)S(1)} custom-call(bf16[1024,1024]{1,0:T(8,128)(2,1)S(1)} %maximum_bitcast_fusion.basis, bf16[384,1024]{1,0:T(8,128)(2,1)S(1)} %pad_maximum_fusion.2.first, bf16[384,1024]{1,0:T(8,128)(2,1)S(1)} %pad_maximum_fusion.3.second), custom_call_target="tpu_custom_call" | custom-call | flops 1 | bytes 1 | tf_op jit(solution)/shard_map/rotate_in/pallas_call | solution.py:145
  58.7 2.0 %collective-permute-done.7.first = bf16[384,1024]{1,0:T(8,128)(2,1)S(1)} collective-permute-done((bf16[384,1024]{1,0:T(8,128)(2,1)S(1)}, bf16[384,1024]{1,0:T(8,128)(2,1)S(1)}, u32[]{:S(2)}, u32[]{:S(2)}) %collective-permute-start.7) | collective-permute-done | bytes 786464 | tf_op jit(solution)/shard_map/ppermute | solution.py:15
  62.5 2.9 %rotate_in.3.late = bf16[1024,768]{1,0:T(8,128)(2,1)S(1)} custom-call(bf16[1024,1024]{1,0:T(8,128)(2,1)S(1)} %maximum_bitcast_fusion.basis, bf16[384,1024]{1,0:T(8,128)(2,1)S(1)} %collective-permute-done.7.first, bf16[384,1024]{1,0:T(8,128)(2,1)S(1)} %collective-permute-done.6.second), custom_call_target="tpu_custom_call" | custom-call | flops 1 | bytes 1 | tf_op jit(solution)/shard_map/rotate_in/pallas_call | solution.py:145
  65.4 4.0 %collective-permute-start.12 = (bf16[1024,768]{1,0:T(8,128)(2,1)S(1)}, bf16[1024,768]{1,0:T(8,128)(2,1)}, u32[]{:S(2)}, u32[]{:S(2)}) collective-permute-start(bf16[1024,768]{1,0:T(8,128)(2,1)S(1)} %rotate_in.3.late), channel_id=1, source_target_pairs={{0,8},{8,0},{1,9},{9,1},{2,10},{10,2},{3,11},{11,3},{4,12},{12,4},... | collective-permute-start | bytes 4718600 | tf_op jit(solution)/shard_map/ppermute | solution.py:23
  70.9 2.5 %collective-permute-start.14 = (bf16[768,384]{1,0:T(8,128)(2,1)}, bf16[768,384]{1,0:T(8,128)(2,1)}, u32[]{:S(2)}, u32[]{:S(2)}) collective-permute-start(bf16[768,384]{1,0:T(8,128)(2,1)} %get-tuple-element.86), channel_id=1, source_target_pairs={{0,96},{32,0},{64,32},{96,64},{1,97},{33,1},{65,33},{97,65},{2,98}... | collective-permute-start | bytes 1769480 | tf_op jit(solution)/shard_map/ppermute | solution.py:19
  74.8 7.2 %contract.4 = (f32[2,512,256]{2,1,0:T(8,128)}, bf16[2,512,256]{2,1,0:T(8,128)(2,1)}) custom-call(s32[1]{0:T(128)} %bitcast.place, bf16[1024,768]{1,0:T(8,128)(2,1)} %copy-done, bf16[1024,768]{1,0:T(8,128)(2,1)} %collective-permute-done.11.early_far, bf16[1024,768]{1,0:T(8,128)(2,1)} %copy-done.1, bf16[1024,768]{1,0:T(8,128)(2,1)} %collective-permute-done.12.late_far, ...), custom_call_target="tpu_custom_call" | custom-call | flops 1 | bytes 1 | tf_op jit(solution)/shard_map/contract/pallas_call | solution.py:216
  82.0 3.4 %collective-permute-start.17 = (bf16[2,512,256]{2,1,0:T(8,128)(2,1)}, bf16[2,512,256]{2,1,0:T(8,128)(2,1)S(1)}, u32[]{:S(2)}, u32[]{:S(2)}) collective-permute-start(bf16[2,512,256]{2,1,0:T(8,128)(2,1)} %get-tuple-element.87), channel_id=1, source_target_pairs={{0,16},{16,0},{1,17},{17,1},{2,18},{18,2},{3,19},{19,3},{4,20},{20... | collective-permute-start | bytes 1572872 | tf_op jit(solution)/shard_map/ppermute | solution.py:23
  87.9 2.7 %collective-permute-start.16 = (bf16[768,384]{1,0:T(8,128)(2,1)S(1)}, bf16[768,384]{1,0:T(8,128)(2,1)S(1)}, u32[]{:S(2)}, u32[]{:S(2)}) collective-permute-start(bf16[768,384]{1,0:T(8,128)(2,1)S(1)} %get-tuple-element.91), channel_id=1, source_target_pairs={{0,96},{32,0},{64,32},{96,64},{1,97},{33,1},{65,33},{97,65},{2,98}... | collective-permute-start | bytes 1769480 | tf_op jit(solution)/shard_map/ppermute | solution.py:19
  90.6 7.0 %collective-permute-done.17 = bf16[2,512,256]{2,1,0:T(8,128)(2,1)S(1)} collective-permute-done((bf16[2,512,256]{2,1,0:T(8,128)(2,1)}, bf16[2,512,256]{2,1,0:T(8,128)(2,1)S(1)}, u32[]{:S(2)}, u32[]{:S(2)}) %collective-permute-start.17) | collective-permute-done | bytes 524320 | tf_op jit(solution)/shard_map/ppermute | solution.py:23
  98.5 2.6 %collective-permute-start.18 = (bf16[512,256]{1,0:T(8,128)(2,1)}, bf16[512,256]{1,0:T(8,128)(2,1)}, u32[]{:S(2)}, u32[]{:S(2)}) collective-permute-start(bf16[512,256]{1,0:T(8,128)(2,1)} %fusion.22), channel_id=1, source_target_pairs={{0,16},{16,0},{1,17},{17,1},{2,18},{18,2},{3,19},{19,3},{4,20},{20... | collective-permute-start | bytes 786440 | tf_op jit(solution)/shard_map/ppermute | solution.py:23
  101.2 7.2 %contract.5 = (f32[2,512,256]{2,1,0:T(8,128)}, bf16[2,512,256]{2,1,0:T(8,128)(2,1)}) custom-call(s32[1]{0:T(128)} %bitcast.place, bf16[1024,768]{1,0:T(8,128)(2,1)} %copy-done, bf16[1024,768]{1,0:T(8,128)(2,1)} %collective-permute-done.11.early_far, bf16[1024,768]{1,0:T(8,128)(2,1)} %copy-done.1, bf16[1024,768]{1,0:T(8,128)(2,1)} %collective-permute-done.12.late_far, ...), custom_call_target="tpu_custom_call" | custom-call | flops 1 | bytes 1 | tf_op jit(solution)/shard_map/contract/pallas_call | solution.py:216
  111.6 2.7 %collective-permute-start.20 = (bf16[768,128]{1,0:T(8,128)(2,1)}, bf16[768,128]{1,0:T(8,128)(2,1)S(1)}, u32[]{:S(2)}, u32[]{:S(2)}) collective-permute-start(bf16[768,128]{1,0:T(8,128)(2,1)} %get-tuple-element.99), channel_id=1, source_target_pairs={{0,96},{32,0},{64,32},{96,64},{1,97},{33,1},{65,33},{97,65},{2,98}... | collective-permute-start | bytes 589832 | tf_op jit(solution)/shard_map/ppermute | solution.py:19
  114.3 7.3 %contract.6 = (f32[2,512,256]{2,1,0:T(8,128)}, bf16[2,512,256]{2,1,0:T(8,128)(2,1)}) custom-call(s32[1]{0:T(128)} %bitcast.place, bf16[1024,768]{1,0:T(8,128)(2,1)} %copy-done, bf16[1024,768]{1,0:T(8,128)(2,1)} %collective-permute-done.11.early_far, bf16[1024,768]{1,0:T(8,128)(2,1)} %copy-done.1, bf16[1024,768]{1,0:T(8,128)(2,1)} %collective-permute-done.12.late_far, ...), custom_call_target="tpu_custom_call" | custom-call | flops 1 | bytes 1 | tf_op jit(solution)/shard_map/contract/pallas_call | solution.py:216
  121.6 2.9 %collective-permute-start.24 = (bf16[2,512,256]{2,1,0:T(8,128)(2,1)}, bf16[2,512,256]{2,1,0:T(8,128)(2,1)S(1)}, u32[]{:S(2)}, u32[]{:S(2)}) collective-permute-start(bf16[2,512,256]{2,1,0:T(8,128)(2,1)} %get-tuple-element.100), channel_id=1, source_target_pairs={{0,16},{16,0},{1,17},{17,1},{2,18},{18,2},{3,19},{19,3},{4,20},{20... | collective-permute-start | bytes 1572872 | tf_op jit(solution)/shard_map/ppermute | solution.py:23
  127.9 7.2 %contract.7 = (f32[2,512,256]{2,1,0:T(8,128)}, bf16[2,512,256]{2,1,0:T(8,128)(2,1)}) custom-call(s32[1]{0:T(128)} %bitcast.place, bf16[1024,768]{1,0:T(8,128)(2,1)} %copy-done, bf16[1024,768]{1,0:T(8,128)(2,1)} %collective-permute-done.11.early_far, bf16[1024,768]{1,0:T(8,128)(2,1)} %copy-done.1, bf16[1024,768]{1,0:T(8,128)(2,1)} %collective-permute-done.12.late_far, ...), custom_call_target="tpu_custom_call" | custom-call | flops 1 | bytes 1 | tf_op jit(solution)/shard_map/contract/pallas_call | solution.py:216
  136.9 2.7 %collective-permute-start.26 = (bf16[512,256]{1,0:T(8,128)(2,1)S(1)}, bf16[512,256]{1,0:T(8,128)(2,1)S(1)}, u32[]{:S(2)}, u32[]{:S(2)}) collective-permute-start(bf16[512,256]{1,0:T(8,128)(2,1)S(1)} %fusion.10), channel_id=1, source_target_pairs={{0,16},{16,0},{1,17},{17,1},{2,18},{18,2},{3,19},{19,3},{4,20},{20... | collective-permute-start | bytes 786440 | tf_op jit(solution)/shard_map/ppermute | solution.py:23
  140.4 7.4 %collective-permute-done.22 = bf16[2,512,256]{2,1,0:T(8,128)(2,1)S(1)} collective-permute-done((bf16[2,512,256]{2,1,0:T(8,128)(2,1)}, bf16[2,512,256]{2,1,0:T(8,128)(2,1)S(1)}, u32[]{:S(2)}, u32[]{:S(2)}) %collective-permute-start.22) | collective-permute-done | bytes 524320 | tf_op jit(solution)/shard_map/ppermute | solution.py:23
  148.4 6.7 %collective-permute-start.27 = (f32[256,1024]{1,0:T(8,128)S(1)}, f32[256,1024]{1,0:T(8,128)S(1)}, u32[]{:S(2)}, u32[]{:S(2)}) collective-permute-start(f32[256,1024]{1,0:T(8,128)S(1)} %get-tuple-element.118), channel_id=1, source_target_pairs={{0,8},{8,0},{1,9},{9,1},{2,10},{10,2},{3,11},{11,3},{4,12},{12,4},... | collective-permute-start | bytes 3145736 | tf_op jit(solution)/shard_map/ppermute | solution.py:23
  156.0 3.0 %collective-permute-done.25 = bf16[512,256]{1,0:T(8,128)(2,1)S(1)} collective-permute-done((bf16[512,256]{1,0:T(8,128)(2,1)S(1)}, bf16[512,256]{1,0:T(8,128)(2,1)S(1)}, u32[]{:S(2)}, u32[]{:S(2)}) %collective-permute-start.25) | collective-permute-done | bytes 262176 | tf_op jit(solution)/shard_map/ppermute | solution.py:23
  161.1 3.5 %collective-permute-done.23 = bf16[512,256]{1,0:T(8,128)(2,1)S(1)} collective-permute-done((bf16[512,256]{1,0:T(8,128)(2,1)S(1)}, bf16[512,256]{1,0:T(8,128)(2,1)S(1)}, u32[]{:S(2)}, u32[]{:S(2)}) %collective-permute-start.23) | collective-permute-done | bytes 262176 | tf_op jit(solution)/shard_map/ppermute | solution.py:23
  167.8 3.9 %collective-permute-start.28 = (bf16[256,1024]{1,0:T(8,128)(2,1)S(1)}, bf16[256,1024]{1,0:T(8,128)(2,1)S(1)}, u32[]{:S(2)}, u32[]{:S(2)}) collective-permute-start(bf16[256,1024]{1,0:T(8,128)(2,1)S(1)} %natural.3), channel_id=1, source_target_pairs={{0,8},{8,0},{1,9},{9,1},{2,10},{10,2},{3,11},{11,3},{4,12},{12,4},... | collective-permute-start | bytes 1572872 | tf_op jit(solution)/shard_map/ppermute | solution.py:23
  (116 shorter events, 39.7 us)
Async XLA Ops:
  2.6 14.1 %collective-permute-start.1 = (bf16[384,1024]{1,0:T(8,128)(2,1)}, bf16[384,1024]{1,0:T(8,128)(2,1)S(1)}, u32[]{:S(2)}, u32[]{:S(2)}) collective-permute-start(bf16[384,1024]{1,0:T(8,128)(2,1)} %partner_columns.1), channel_id=1, source_target_pairs={{0,8},{8,0},{1,9},{9,1},{2,10},{10,2},{3,11},{11,3},{4,12},{12,4},... | collective-permute-start | bytes 2359304 | tf_op jit(solution)/shard_map/ppermute | solution.py:23
  4.0 17.8 %collective-permute-start = (bf16[384,512]{1,0:T(8,128)(2,1)}, bf16[384,512]{1,0:T(8,128)(2,1)}, u32[]{:S(2)}, u32[]{:S(2)}) collective-permute-start(bf16[384,512]{1,0:T(8,128)(2,1)} %param.4), channel_id=1, source_target_pairs={{0,0},{2,32},{4,64},{6,96},{32,2},{34,34},{36,66},{38,98},{64,4},{... | collective-permute-start | bytes 1179656 | tf_op jit(solution)/shard_map/ppermute | solution.py:27
  21.8 33.9 %copy-start.8 = (bf16[768,256]{1,0:T(8,128)(2,1)}, bf16[768,256]{1,0:T(8,128)(2,1)S(1)}, u32[]{:S(2)}) copy-start(bf16[768,256]{1,0:T(8,128)(2,1)S(1)} %get-tuple-element.92.refs_0_.own) | copy-start | bytes 1179652
  21.8 47.7 %copy-start.7 = (bf16[768,256]{1,0:T(8,128)(2,1)}, bf16[768,256]{1,0:T(8,128)(2,1)S(1)}, u32[]{:S(2)}) copy-start(bf16[768,256]{1,0:T(8,128)(2,1)S(1)} %get-tuple-element.84.refs_0_.own) | copy-start | bytes 1179652
  21.8 64.9 %copy-start.6 = (bf16[768,256]{1,0:T(8,128)(2,1)}, bf16[768,256]{1,0:T(8,128)(2,1)S(1)}, u32[]{:S(2)}) copy-start(bf16[768,256]{1,0:T(8,128)(2,1)S(1)} %get-tuple-element.81.refs_0_.own) | copy-start | bytes 1179652
  21.9 15.4 %collective-permute-start.3 = (bf16[384,512]{1,0:T(8,128)(2,1)}, bf16[384,512]{1,0:T(8,128)(2,1)S(1)}, u32[]{:S(2)}, u32[]{:S(2)}) collective-permute-start(bf16[384,512]{1,0:T(8,128)(2,1)} %collective-permute-done), channel_id=1, source_target_pairs={{0,4},{2,6},{4,0},{6,2},{1,5},{3,7},{5,1},{7,3},{8,12},{10,14},{12... | collective-permute-start | bytes 1179656 | tf_op jit(solution)/shard_map/ppermute | solution.py:15
  28.8 9.7 %collective-permute-start.2 = (bf16[384,512]{1,0:T(8,128)(2,1)}, bf16[384,512]{1,0:T(8,128)(2,1)S(1)}, u32[]{:S(2)}, u32[]{:S(2)}) collective-permute-start(bf16[384,512]{1,0:T(8,128)(2,1)} %collective-permute-done), channel_id=1, source_target_pairs={{0,1},{1,0},{2,3},{3,2},{4,5},{5,4},{6,7},{7,6},{8,9},{9,8},{10,11... | collective-permute-start | bytes 1179656 | tf_op jit(solution)/shard_map/ppermute | solution.py:23
  30.4 9.5 %collective-permute-start.5 = (bf16[768,256]{1,0:T(8,128)(2,1)S(1)}, bf16[768,256]{1,0:T(8,128)(2,1)S(1)}, u32[]{:S(2)}, u32[]{:S(2)}) collective-permute-start(bf16[768,256]{1,0:T(8,128)(2,1)S(1)} %get-tuple-element.64.own), channel_id=1, source_target_pairs={{0,96},{32,0},{64,32},{96,64},{1,97},{33,1},{65,33},{97,65},{2,98}... | collective-permute-start | bytes 1179656 | tf_op jit(solution)/shard_map/ppermute | solution.py:19
  33.1 9.9 %collective-permute-start.4 = (bf16[768,256]{1,0:T(8,128)(2,1)S(1)}, bf16[768,256]{1,0:T(8,128)(2,1)S(1)}, u32[]{:S(2)}, u32[]{:S(2)}) collective-permute-start(bf16[768,256]{1,0:T(8,128)(2,1)S(1)} %get-tuple-element.64.own), channel_id=1, source_target_pairs={{0,32},{32,64},{64,96},{96,0},{1,33},{33,65},{65,97},{97,1},{2,34}... | collective-permute-start | bytes 1179656 | tf_op jit(solution)/shard_map/ppermute | solution.py:19
  44.4 16.3 %collective-permute-start.7 = (bf16[384,1024]{1,0:T(8,128)(2,1)S(1)}, bf16[384,1024]{1,0:T(8,128)(2,1)S(1)}, u32[]{:S(2)}, u32[]{:S(2)}) collective-permute-start(bf16[384,1024]{1,0:T(8,128)(2,1)S(1)} %pad_maximum_fusion.2.first), channel_id=1, source_target_pairs={{0,6},{2,0},{4,2},{6,4},{1,7},{3,1},{5,3},{7,5},{8,14},{10,8},{12,... | collective-permute-start | bytes 2359304 | tf_op jit(solution)/shard_map/ppermute | solution.py:15
  44.8 17.6 %collective-permute-start.6 = (bf16[384,1024]{1,0:T(8,128)(2,1)S(1)}, bf16[384,1024]{1,0:T(8,128)(2,1)S(1)}, u32[]{:S(2)}, u32[]{:S(2)}) collective-permute-start(bf16[384,1024]{1,0:T(8,128)(2,1)S(1)} %pad_maximum_fusion.2.first), channel_id=1, source_target_pairs={{0,2},{2,4},{4,6},{6,0},{1,3},{3,5},{5,7},{7,1},{8,10},{10,12},{12... | collective-permute-start | bytes 2359304 | tf_op jit(solution)/shard_map/ppermute | solution.py:15
  46.0 12.6 %collective-permute-start.9 = (bf16[768,384]{1,0:T(8,128)(2,1)S(1)}, bf16[768,384]{1,0:T(8,128)(2,1)S(1)}, u32[]{:S(2)}, u32[]{:S(2)}) collective-permute-start(bf16[768,384]{1,0:T(8,128)(2,1)S(1)} %get-tuple-element.76), channel_id=1, source_target_pairs={{0,32},{32,64},{64,96},{96,0},{1,33},{33,65},{65,97},{97,1},{2,34}... | collective-permute-start | bytes 1769480 | tf_op jit(solution)/shard_map/ppermute | solution.py:19
  46.0 12.7 %collective-permute-start.10 = (bf16[768,384]{1,0:T(8,128)(2,1)S(1)}, bf16[768,384]{1,0:T(8,128)(2,1)S(1)}, u32[]{:S(2)}, u32[]{:S(2)}) collective-permute-start(bf16[768,384]{1,0:T(8,128)(2,1)S(1)} %get-tuple-element.77), channel_id=1, source_target_pairs={{0,96},{32,0},{64,32},{96,64},{1,97},{33,1},{65,33},{97,65},{2,98}... | collective-permute-start | bytes 1769480 | tf_op jit(solution)/shard_map/ppermute | solution.py:19
  48.7 6.9 %collective-permute-start.8 = (bf16[384,512]{1,0:T(8,128)(2,1)S(1)}, bf16[384,512]{1,0:T(8,128)(2,1)S(1)}, u32[]{:S(2)}, u32[]{:S(2)}) collective-permute-start(bf16[384,512]{1,0:T(8,128)(2,1)S(1)} %collective-permute-done.3), channel_id=1, source_target_pairs={{0,1},{1,0},{2,3},{3,2},{4,5},{5,4},{6,7},{7,6},{8,9},{9,8},{10,11... | collective-permute-start | bytes 1179656 | tf_op jit(solution)/shard_map/ppermute | solution.py:23
  65.4 8.0 %collective-permute-start.12 = (bf16[1024,768]{1,0:T(8,128)(2,1)S(1)}, bf16[1024,768]{1,0:T(8,128)(2,1)}, u32[]{:S(2)}, u32[]{:S(2)}) collective-permute-start(bf16[1024,768]{1,0:T(8,128)(2,1)S(1)} %rotate_in.3.late), channel_id=1, source_target_pairs={{0,8},{8,0},{1,9},{9,1},{2,10},{10,2},{3,11},{11,3},{4,12},{12,4},... | collective-permute-start | bytes 4718600 | tf_op jit(solution)/shard_map/ppermute | solution.py:23
  69.4 5.4 %collective-permute-start.11 = (bf16[1024,768]{1,0:T(8,128)(2,1)S(1)}, bf16[1024,768]{1,0:T(8,128)(2,1)}, u32[]{:S(2)}, u32[]{:S(2)}) collective-permute-start(bf16[1024,768]{1,0:T(8,128)(2,1)S(1)} %rotate_in.2.early), channel_id=1, source_target_pairs={{0,8},{8,0},{1,9},{9,1},{2,10},{10,2},{3,11},{11,3},{4,12},{12,4},... | collective-permute-start | bytes 4718600 | tf_op jit(solution)/shard_map/ppermute | solution.py:23
  70.7 16.0 %collective-permute-start.13 = (bf16[768,384]{1,0:T(8,128)(2,1)}, bf16[768,384]{1,0:T(8,128)(2,1)}, u32[]{:S(2)}, u32[]{:S(2)}) collective-permute-start(bf16[768,384]{1,0:T(8,128)(2,1)} %get-tuple-element.85), channel_id=1, source_target_pairs={{0,32},{32,64},{64,96},{96,0},{1,33},{33,65},{65,97},{97,1},{2,34}... | collective-permute-start | bytes 1769480 | tf_op jit(solution)/shard_map/ppermute | solution.py:19
  70.9 15.8 %collective-permute-start.14 = (bf16[768,384]{1,0:T(8,128)(2,1)}, bf16[768,384]{1,0:T(8,128)(2,1)}, u32[]{:S(2)}, u32[]{:S(2)}) collective-permute-start(bf16[768,384]{1,0:T(8,128)(2,1)} %get-tuple-element.86), channel_id=1, source_target_pairs={{0,96},{32,0},{64,32},{96,64},{1,97},{33,1},{65,33},{97,65},{2,98}... | collective-permute-start | bytes 1769480 | tf_op jit(solution)/shard_map/ppermute | solution.py:19
  82.0 15.6 %collective-permute-start.17 = (bf16[2,512,256]{2,1,0:T(8,128)(2,1)}, bf16[2,512,256]{2,1,0:T(8,128)(2,1)S(1)}, u32[]{:S(2)}, u32[]{:S(2)}) collective-permute-start(bf16[2,512,256]{2,1,0:T(8,128)(2,1)} %get-tuple-element.87), channel_id=1, source_target_pairs={{0,16},{16,0},{1,17},{17,1},{2,18},{18,2},{3,19},{19,3},{4,20},{20... | collective-permute-start | bytes 1572872 | tf_op jit(solution)/shard_map/ppermute | solution.py:23
  87.9 21.0 %collective-permute-start.15 = (bf16[768,384]{1,0:T(8,128)(2,1)S(1)}, bf16[768,384]{1,0:T(8,128)(2,1)S(1)}, u32[]{:S(2)}, u32[]{:S(2)}) collective-permute-start(bf16[768,384]{1,0:T(8,128)(2,1)S(1)} %get-tuple-element.90), channel_id=1, source_target_pairs={{0,32},{32,64},{64,96},{96,0},{1,33},{33,65},{65,97},{97,1},{2,34}... | collective-permute-start | bytes 1769480 | tf_op jit(solution)/shard_map/ppermute | solution.py:19
  87.9 20.9 %collective-permute-start.16 = (bf16[768,384]{1,0:T(8,128)(2,1)S(1)}, bf16[768,384]{1,0:T(8,128)(2,1)S(1)}, u32[]{:S(2)}, u32[]{:S(2)}) collective-permute-start(bf16[768,384]{1,0:T(8,128)(2,1)S(1)} %get-tuple-element.91), channel_id=1, source_target_pairs={{0,96},{32,0},{64,32},{96,64},{1,97},{33,1},{65,33},{97,65},{2,98}... | collective-permute-start | bytes 1769480 | tf_op jit(solution)/shard_map/ppermute | solution.py:19
  98.5 10.3 %collective-permute-start.18 = (bf16[512,256]{1,0:T(8,128)(2,1)}, bf16[512,256]{1,0:T(8,128)(2,1)}, u32[]{:S(2)}, u32[]{:S(2)}) collective-permute-start(bf16[512,256]{1,0:T(8,128)(2,1)} %fusion.22), channel_id=1, source_target_pairs={{0,16},{16,0},{1,17},{17,1},{2,18},{18,2},{3,19},{19,3},{4,20},{20... | collective-permute-start | bytes 786440 | tf_op jit(solution)/shard_map/ppermute | solution.py:23
  108.4 18.8 %collective-permute-start.21 = (bf16[2,512,256]{2,1,0:T(8,128)(2,1)}, bf16[2,512,256]{2,1,0:T(8,128)(2,1)}, u32[]{:S(2)}, u32[]{:S(2)}) collective-permute-start(bf16[2,512,256]{2,1,0:T(8,128)(2,1)} %get-tuple-element.93), channel_id=1, source_target_pairs={{0,16},{16,0},{1,17},{17,1},{2,18},{18,2},{3,19},{19,3},{4,20},{20... | collective-permute-start | bytes 1572872 | tf_op jit(solution)/shard_map/ppermute | solution.py:23
  111.6 15.5 %collective-permute-start.19 = (bf16[768,128]{1,0:T(8,128)(2,1)}, bf16[768,128]{1,0:T(8,128)(2,1)S(1)}, u32[]{:S(2)}, u32[]{:S(2)}) collective-permute-start(bf16[768,128]{1,0:T(8,128)(2,1)} %get-tuple-element.98), channel_id=1, source_target_pairs={{0,32},{32,64},{64,96},{96,0},{1,33},{33,65},{65,97},{97,1},{2,34}... | collective-permute-start | bytes 589832 | tf_op jit(solution)/shard_map/ppermute | solution.py:19
  111.6 15.5 %collective-permute-start.20 = (bf16[768,128]{1,0:T(8,128)(2,1)}, bf16[768,128]{1,0:T(8,128)(2,1)S(1)}, u32[]{:S(2)}, u32[]{:S(2)}) collective-permute-start(bf16[768,128]{1,0:T(8,128)(2,1)} %get-tuple-element.99), channel_id=1, source_target_pairs={{0,96},{32,0},{64,32},{96,64},{1,97},{33,1},{65,33},{97,65},{2,98}... | collective-permute-start | bytes 589832 | tf_op jit(solution)/shard_map/ppermute | solution.py:19
  121.6 18.1 %collective-permute-start.24 = (bf16[2,512,256]{2,1,0:T(8,128)(2,1)}, bf16[2,512,256]{2,1,0:T(8,128)(2,1)S(1)}, u32[]{:S(2)}, u32[]{:S(2)}) collective-permute-start(bf16[2,512,256]{2,1,0:T(8,128)(2,1)} %get-tuple-element.100), channel_id=1, source_target_pairs={{0,16},{16,0},{1,17},{17,1},{2,18},{18,2},{3,19},{19,3},{4,20},{20... | collective-permute-start | bytes 1572872 | tf_op jit(solution)/shard_map/ppermute | solution.py:23
  135.1 12.6 %collective-permute-start.22 = (bf16[2,512,256]{2,1,0:T(8,128)(2,1)}, bf16[2,512,256]{2,1,0:T(8,128)(2,1)S(1)}, u32[]{:S(2)}, u32[]{:S(2)}) collective-permute-start(bf16[2,512,256]{2,1,0:T(8,128)(2,1)} %get-tuple-element.104), channel_id=1, source_target_pairs={{0,16},{16,0},{1,17},{17,1},{2,18},{18,2},{3,19},{19,3},{4,20},{20... | collective-permute-start | bytes 1572872 | tf_op jit(solution)/shard_map/ppermute | solution.py:23
  136.9 18.2 %collective-permute-start.26 = (bf16[512,256]{1,0:T(8,128)(2,1)S(1)}, bf16[512,256]{1,0:T(8,128)(2,1)S(1)}, u32[]{:S(2)}, u32[]{:S(2)}) collective-permute-start(bf16[512,256]{1,0:T(8,128)(2,1)S(1)} %fusion.10), channel_id=1, source_target_pairs={{0,16},{16,0},{1,17},{17,1},{2,18},{18,2},{3,19},{19,3},{4,20},{20... | collective-permute-start | bytes 786440 | tf_op jit(solution)/shard_map/ppermute | solution.py:23
  139.9 19.0 %collective-permute-start.25 = (bf16[512,256]{1,0:T(8,128)(2,1)S(1)}, bf16[512,256]{1,0:T(8,128)(2,1)S(1)}, u32[]{:S(2)}, u32[]{:S(2)}) collective-permute-start(bf16[512,256]{1,0:T(8,128)(2,1)S(1)} %fusion.14), channel_id=1, source_target_pairs={{0,16},{16,0},{1,17},{17,1},{2,18},{18,2},{3,19},{19,3},{4,20},{20... | collective-permute-start | bytes 786440 | tf_op jit(solution)/shard_map/ppermute | solution.py:23
  148.4 11.3 %collective-permute-start.27 = (f32[256,1024]{1,0:T(8,128)S(1)}, f32[256,1024]{1,0:T(8,128)S(1)}, u32[]{:S(2)}, u32[]{:S(2)}) collective-permute-start(f32[256,1024]{1,0:T(8,128)S(1)} %get-tuple-element.118), channel_id=1, source_target_pairs={{0,8},{8,0},{1,9},{9,1},{2,10},{10,2},{3,11},{11,3},{4,12},{12,4},... | collective-permute-start | bytes 3145736 | tf_op jit(solution)/shard_map/ppermute | solution.py:23
  155.9 8.7 %collective-permute-start.23 = (bf16[512,256]{1,0:T(8,128)(2,1)S(1)}, bf16[512,256]{1,0:T(8,128)(2,1)S(1)}, u32[]{:S(2)}, u32[]{:S(2)}) collective-permute-start(bf16[512,256]{1,0:T(8,128)(2,1)S(1)} %fusion.18), channel_id=1, source_target_pairs={{0,16},{16,0},{1,17},{17,1},{2,18},{18,2},{3,19},{19,3},{4,20},{20... | collective-permute-start | bytes 786440 | tf_op jit(solution)/shard_map/ppermute | solution.py:23
  167.8 5.5 %collective-permute-start.28 = (bf16[256,1024]{1,0:T(8,128)(2,1)S(1)}, bf16[256,1024]{1,0:T(8,128)(2,1)S(1)}, u32[]{:S(2)}, u32[]{:S(2)}) collective-permute-start(bf16[256,1024]{1,0:T(8,128)(2,1)S(1)} %natural.3), channel_id=1, source_target_pairs={{0,8},{8,0},{1,9},{9,1},{2,10},{10,2},{3,11},{11,3},{4,12},{12,4},... | collective-permute-start | bytes 1572872 | tf_op jit(solution)/shard_map/ppermute | solution.py:23
  (19 other events, 151.7 us)

commit v2 on v1

--- a/solution.py
+++ b/solution.py
@@ -1,3 +1,4 @@
+import functools
 import math
 
 import jax
@@ -154,12 +155,12 @@
     )(basis, first, second)
 
 
-def contract_kernel(place, early, early_far, late, late_far, own, above, below, right, left, *refs):
+def contract_kernel(part, place, early, early_far, late, late_far, own, above, below, right, left, *refs):
     kept, send, features, grads, feature_sems, grad_sems = refs
     tokens = features.shape[2] // 2
-    columns = grads.shape[2]
-    half = columns // 2
+    half = own.shape[1] // 2
     rows = kept.shape[1]
+    halves = range(2) if part is None else (part,)
 
     def feature_copies(e, index, sources):
         for far, source in enumerate(sources):
@@ -171,14 +172,18 @@
             )
 
     def grad_copies(e):
-        if e == 2:
-            start = right.shape[1] - half
-            pairs = [(right.at[:, pl.ds(start, half)], 0), (left.at[:, pl.ds(start, half)], half)]
-        else:
-            source = {0: own, 1: above, 3: below}[e]
-            pairs = [(source.at[:, pl.ds(k * half, half)], k * half) for k in range(2)]
-        for k, (source, start) in enumerate(pairs):
-            yield pltpu.make_async_copy(source, grads.at[e, :, pl.ds(start, half)], grad_sems.at[e, k])
+        for slot, k in enumerate(halves):
+            if e == 2:
+                source = (right, left)[k]
+                start = source.shape[1] - half
+            else:
+                source = {0: own, 1: above, 3: below}[e]
+                start = k * half
+            yield pltpu.make_async_copy(
+                source.at[:, pl.ds(start, half)],
+                grads.at[e, :, pl.ds(slot * half, half)],
+                grad_sems.at[e, slot],
+            )
 
     for e in range(4):
         index = (place[0] + e) % 4
@@ -197,9 +202,9 @@
             copy.wait()
         for copy in feature_copies(e, 0, (early, early_far)):
             copy.wait()
-        part, values = features[e], grads[e]
-        grad = dot(part, values)
-        scale = dot(squared(part), squared(values))
+        rotated_in, values = features[e], grads[e]
+        grad = dot(rotated_in, values)
+        scale = dot(squared(rotated_in), squared(values))
         grad_part = grad if e == 0 else grad_part + grad
         scale_part = scale if e == 0 else scale_part + scale
     kept[0] = scale_part[:rows]
@@ -208,13 +213,14 @@
     send[1] = grad_part[rows:].astype(send.dtype)
 
 
-def contracted(place, lefts, own, brought, following):
+def contracted(place, lefts, own, brought, following, part=None):
     features, depth = lefts[0].shape
     tokens, columns = own.shape
+    columns = columns if part is None else columns // 2
     rows = features // 2
     out_spec = pl.BlockSpec((2, rows, columns), lambda i, s: (0, 0, 0))
     return pl.pallas_call(
-        contract_kernel,
+        functools.partial(contract_kernel, part),
         grid_spec=pltpu.PrefetchScalarGridSpec(
             num_scalar_prefetch=1,
             grid=(1,),
@@ -323,13 +329,11 @@
     other = swap(mine, "z_lo")
     two = along_y(mine, 2)
     first = around_x(own_out[0], own_out[0])
-    mine, other, two, *first = fence(mine, other, two, *first)
+    mine, other, two = fence(mine, other, two)
 
     whole = jnp.concatenate([mine, other], 1)
-    sent = payloads(own_out[1], columns, *first)
-    whole, two, *sent = fence(whole, two, *sent)
     below, above = along_y(whole, 1), along_y(whole, -1)
-    second = around_x(*sent)
+    second = around_x(*payloads(own_out[1], columns, *first))
     two = jnp.concatenate([two, swap(two, "z_lo")], 1)
     early = rotated(basis_turn, whole, two)
     below, above, early, *second = fence(below, above, early, *second)
@@ -348,19 +352,25 @@
     third = around_x(*payloads(own_out[2], columns, *second))
     late = rotated(basis_turn, above, below)
     lefts = [early, swap(early, "core"), late, swap(late, "core")]
-    kept0, send0 = contracted(turn, lefts, own_out[0], first, second)
-    got0 = swap(send0, "z_hi")
-    *third, send0 = fence(*third, send0)
+    kept0, send0 = contracted(turn, lefts, own_out[0], first, second, 0)
+    own0, send0 = fence(own_out[0], send0)
+    kept0b, send0b = contracted(turn, lefts, own0, first, second, 1)
+    got0, got0b = swap(send0, "z_hi"), swap(send0b, "z_hi")
+    *third, send0b = fence(*third, send0b)
     fourth = around_x(*payloads(own_out[3], columns, *third))
     own1, got0 = fence(own_out[1], got0)
     kept1, send1 = contracted(turn, lefts, own1, second, third)
     got1 = swap(send1, "z_hi")
     scales0, turned0 = finished(kept0, got0)
-    *fourth, send1, over0 = fence(*fourth, send1, swap(turned0, "z_hi"))
+    scales0b, turned0b = finished(kept0b, got0b)
+    scales0 = jnp.concatenate([scales0, scales0b], 1)
+    turned0 = jnp.concatenate([turned0, turned0b], 1)
+    over0 = swap(turned0, "z_hi")
+    *fourth, send1 = fence(*fourth, send1)
     fifth = around_x(*payloads(None, columns, *fourth, mib=60))
     kept2, send2 = contracted(turn, lefts, own_out[2], third, fourth)
     got2 = swap(send2, "z_hi")
-    *fifth, send2, got1 = fence(*fifth, send2, got1)
+    *fifth, send2, got1, over0 = fence(*fifth, send2, got1, over0)
     kept3, send3 = contracted(turn, lefts, own_out[3], fourth, fifth)
 
     got3 = swap(send3, "z_hi")

time: 175 us -> 170 us (0.971)
  waiting for transfers between devices: 44.3 us -> 30.6 us
  Pallas kernels: 49.2 us -> 56 us
  starting transfers between devices: 57.6 us -> 61.3 us
    ppermute x15 -> x16, waiting for transfers between devices: 30.6 us -> 22.4 us  [swap(): return lax.ppermute(v, axis, [(0, 1), (1, 0)])]
    ppermute x3, starting transfers between devices: 8.45 us -> 15.4 us  [along_y(): return lax.ppermute(v, 'y', [(i, (i + d) % 4) for i in range(4)])]
    pallas_call x4 -> x5, Pallas kernels: 28.8 us -> 35.4 us  [contracted(): pl.pallas_call(functools.partial(contract_kernel, part), grid_spec=pltpu....]
    ppermute x10, waiting for transfers between devices: 5.86 us -> 1.25 us  [along_x(): return lax.ppermute(v, 'x', [(i, (i + d) % 4) for i in range(4)])]
    ppermute x1, starting transfers between devices: 4.48 us -> 1.64 us  [transpose_xy(): lax.ppermute(v, ('x', 'y'), [(x * 4 + y, y * 4 + x) for x in range(4) for...]
    unnamed x44 -> x49, local copies, waits for them, and re-layouts: 4.23 us -> 5.44 us
    ppermute x15 -> x16, starting transfers between devices: 31.2 us -> 31.1 us  [swap(): return lax.ppermute(v, axis, [(0, 1), (1, 0)])]
  transfers between devices with their start and end apart: 29 -> 30, of which waited for: 14 -> 9; matrix products, arithmetic and copies ran while one was open for 9% -> 9% of each run, Pallas kernels for 24% -> 31%
where the time goes in v2:
time: 170 us
  starting transfers between devices  61.3 us (36%)
  Pallas kernels  56 us (33%)
  waiting for transfers between devices  30.6 us (18%)
  local copies, waits for them, and re-layouts  11 us (6%)
  other arithmetic  6.04 us (4%)
  matrix products  3.68 us (2%)
    pallas_call x5, Pallas kernels, contracted(): pl.pallas_call(functools.partial(contract_kernel, part), grid_spec=pltpu....  35.4 us
    ppermute x16, starting transfers between devices, swap(): return lax.ppermute(v, axis, [(0, 1), (1, 0)])  31.1 us
    ppermute x16, waiting for transfers between devices, swap(): return lax.ppermute(v, axis, [(0, 1), (1, 0)])  22.4 us
    ppermute x3, starting transfers between devices, along_y(): return lax.ppermute(v, 'y', [(i, (i + d) % 4) for i in range(4)])  15.4 us
    ppermute x10, starting transfers between devices, along_x(): return lax.ppermute(v, 'x', [(i, (i + d) % 4) for i in range(4)])  13.2 us
    ppermute x3, waiting for transfers between devices, along_y(): return lax.ppermute(v, 'y', [(i, (i + d) % 4) for i in range(4)])  6.94 us
    pallas_call x2, Pallas kernels, rotated(): pl.pallas_call(rotate_kernel, grid=(4,), in_specs=[pl.BlockSpec((tile, de...  5.76 us
    unnamed x49, local copies, waits for them, and re-layouts  5.44 us
  transfers between devices with their start and end apart: 30, of which 9 were waited for; matrix products, arithmetic and copies ran while one was open for 9% of the time, Pallas kernels for 31%

profile of v2, /device:TPU:1, one launch (start us, length us, event | category | flops | bytes accessed | tf_op | source)
XLA Modules:
  0.0 169.8 jit_solution(9216496718694698921)
XLA Ops:
  0.6 2.0 %partner_columns.1 = bf16[384,1024]{1,0:T(8,128)(2,1)} custom-call(s32[1]{0:T(128)} %bitcast.4.place, bf16[384,2048]{1,0:T(8,128)(2,1)} %own.1), custom_call_target="tpu_custom_call" | custom-call | flops 1 | bytes 1 | tf_op jit(solution)/shard_map/partner_columns/pallas_call | solution.py:56
  5.7 2.7 %constant_dynamic-slice_fusion.2 = (bf16[1,1024,512]{2,1,0:T(8,128)(2,1)S(1)}, bf16[1,1024,512]{2,1,0:T(8,128)(2,1)S(1)}) fusion(bf16[4,1024,1024]{2,1,0:T(8,128)(2,1)} %param.6, s32[]{:T(128)S(6)} %select_n.38, s32[]{:T(128)S(6)} %select_n.42, s32[]{:T(128)S(6)} %select_n.40), kind=kLoop, calls=%fused_computation.77 | loop fusion | bytes 4194316 | tf_op jit(solution)/shard_map/dynamic_slice | solution.py:315
  11.0 2.8 %fusion.4 = (bf16[512,1024]{0,1:T(8,128)(2,1)}, bf16[512,1024]{0,1:T(8,128)(2,1)S(1)}, bf16[512,1024]{0,1:T(8,128)(2,1)S(1)}) fusion(s32[]{:T(128)S(6)} %select_n.39, bf16[1024,512]{0,1:T(8,128)(2,1)S(1)} %bitcast.73, bf16[1024,512]{0,1:T(8,128)(2,1)} %bitcast.74, s32[]{:T(128)S(6)} %select_n.43, s32[]{:T(128)S(6)} %select_n.44), kind=kLoop, calls=%fused_computation.15 | loop fusion | flops 6291456 | bytes 5242892 | tf_op jit(solution)/shard_map/concatenate | solution.py:314
  15.2 3.9 %rotate_out.1 = (bf16[768,256]{1,0:T(8,128)(2,1)S(1)}, bf16[768,256]{1,0:T(8,128)(2,1)S(1)}, bf16[768,256]{1,0:T(8,128)(2,1)S(1)}, bf16[768,256]{1,0:T(8,128)(2,1)S(1)}) custom-call(s32[1]{0:T(128)} %bitcast.4.place, bf16[384,2048]{1,0:T(8,128)(2,1)S(1)} %copy-done.5, bf16[384,1024]{1,0:T(8,128)(2,1)S(1)} %collective-permute-done.1.other, ...), custom_call_target="tpu_custom_call" | custom-call | flops 1 | bytes 1 | tf_op jit(solution)/shard_map/rotate_out/pallas_call | solution.py:85
  21.0 9.3 %collective-permute-start.3 = (bf16[384,512]{1,0:T(8,128)(2,1)S(1)}, bf16[384,512]{1,0:T(8,128)(2,1)S(1)}, u32[]{:S(2)}, u32[]{:S(2)}) collective-permute-start(bf16[384,512]{1,0:T(8,128)(2,1)S(1)} %collective-permute-done), channel_id=1, source_target_pairs={{0,4},{2,6},{4,0},{6,2},{1,5},{3,7},{5,1},{7,3},{8,12},{10,14},{12... | collective-permute-start | bytes 1179656 | tf_op jit(solution)/shard_map/ppermute | solution.py:16
  33.0 5.2 %collective-permute-done.3 = bf16[384,512]{1,0:T(8,128)(2,1)S(1)} collective-permute-done((bf16[384,512]{1,0:T(8,128)(2,1)S(1)}, bf16[384,512]{1,0:T(8,128)(2,1)S(1)}, u32[]{:S(2)}, u32[]{:S(2)}) %collective-permute-start.3) | collective-permute-done | bytes 393248 | tf_op jit(solution)/shard_map/ppermute | solution.py:16
  38.3 3.9 %collective-permute-start.4 = (bf16[384,1024]{1,0:T(8,128)(2,1)S(1)}, bf16[384,1024]{1,0:T(8,128)(2,1)S(1)}, u32[]{:S(2)}, u32[]{:S(2)}) collective-permute-start(bf16[384,1024]{1,0:T(8,128)(2,1)S(1)} %constant_dynamic-update-slice_fusion.first), channel_id=1, source_target_pairs={{0,2},{2,4},{4,6},{6,0},{1,3},{3,5},{5,7},{7,1},{8,10},{10,12},{12... | collective-permute-start | bytes 2359304 | tf_op jit(solution)/shard_map/ppermute | solution.py:16
  42.2 2.2 %collective-permute-start.5 = (bf16[384,1024]{1,0:T(8,128)(2,1)S(1)}, bf16[384,1024]{1,0:T(8,128)(2,1)S(1)}, u32[]{:S(2)}, u32[]{:S(2)}) collective-permute-start(bf16[384,1024]{1,0:T(8,128)(2,1)S(1)} %constant_dynamic-update-slice_fusion.first), channel_id=1, source_target_pairs={{0,6},{2,0},{4,2},{6,4},{1,7},{3,1},{5,3},{7,5},{8,14},{10,8},{12,... | collective-permute-start | bytes 2359304 | tf_op jit(solution)/shard_map/ppermute | solution.py:16
  45.2 2.3 %collective-permute-start.10 = (bf16[768,384]{1,0:T(8,128)(2,1)S(1)}, bf16[768,384]{1,0:T(8,128)(2,1)S(1)}, u32[]{:S(2)}, u32[]{:S(2)}) collective-permute-start(bf16[768,384]{1,0:T(8,128)(2,1)S(1)} %get-tuple-element.69), channel_id=1, source_target_pairs={{0,96},{32,0},{64,32},{96,64},{1,97},{33,1},{65,33},{97,65},{2,98}... | collective-permute-start | bytes 1769480 | tf_op jit(solution)/shard_map/ppermute | solution.py:20
  47.7 7.4 %collective-permute-done.6 = bf16[384,512]{1,0:T(8,128)(2,1)S(1)} collective-permute-done((bf16[384,512]{1,0:T(8,128)(2,1)S(1)}, bf16[384,512]{1,0:T(8,128)(2,1)S(1)}, u32[]{:S(2)}, u32[]{:S(2)}) %collective-permute-start.6) | collective-permute-done | bytes 393248 | tf_op jit(solution)/shard_map/ppermute | solution.py:24
  55.2 2.9 %rotate_in.2.early = bf16[1024,768]{1,0:T(8,128)(2,1)S(1)} custom-call(bf16[1024,1024]{1,0:T(8,128)(2,1)S(1)} %maximum_bitcast_fusion.basis, bf16[384,1024]{1,0:T(8,128)(2,1)S(1)} %constant_dynamic-update-slice_fusion.first, bf16[384,1024]{1,0:T(8,128)(2,1)S(1)} %pad_maximum_fusion.1.second), custom_call_target="tpu_custom_call" | custom-call | flops 1 | bytes 1 | tf_op jit(solution)/shard_map/rotate_in/pallas_call | solution.py:146
  60.2 2.6 %collective-permute-start.11 = (bf16[1024,768]{1,0:T(8,128)(2,1)S(1)}, bf16[1024,768]{1,0:T(8,128)(2,1)}, u32[]{:S(2)}, u32[]{:S(2)}) collective-permute-start(bf16[1024,768]{1,0:T(8,128)(2,1)S(1)} %rotate_in.2.early), channel_id=1, source_target_pairs={{0,8},{8,0},{1,9},{9,1},{2,10},{10,2},{3,11},{11,3},{4,12},{12,4},... | collective-permute-start | bytes 4718600 | tf_op jit(solution)/shard_map/ppermute | solution.py:24
  62.8 2.9 %rotate_in.3.late = bf16[1024,768]{1,0:T(8,128)(2,1)S(1)} custom-call(bf16[1024,1024]{1,0:T(8,128)(2,1)S(1)} %maximum_bitcast_fusion.basis, bf16[384,1024]{1,0:T(8,128)(2,1)S(1)} %collective-permute-done.5.first, bf16[384,1024]{1,0:T(8,128)(2,1)S(1)} %collective-permute-done.4.second), custom_call_target="tpu_custom_call" | custom-call | flops 1 | bytes 1 | tf_op jit(solution)/shard_map/rotate_in/pallas_call | solution.py:146
  67.3 2.7 %collective-permute-start.14 = (bf16[768,384]{1,0:T(8,128)(2,1)}, bf16[768,384]{1,0:T(8,128)(2,1)}, u32[]{:S(2)}, u32[]{:S(2)}) collective-permute-start(bf16[768,384]{1,0:T(8,128)(2,1)} %get-tuple-element.78), channel_id=1, source_target_pairs={{0,96},{32,0},{64,32},{96,64},{1,97},{33,1},{65,33},{97,65},{2,98}... | collective-permute-start | bytes 1769480 | tf_op jit(solution)/shard_map/ppermute | solution.py:20
  69.9 6.9 %contract.5 = (f32[2,512,128]{2,1,0:T(8,128)}, bf16[2,512,128]{2,1,0:T(8,128)(2,1)}) custom-call(s32[1]{0:T(128)} %bitcast.place, bf16[1024,768]{1,0:T(8,128)(2,1)} %copy-done, bf16[1024,768]{1,0:T(8,128)(2,1)} %collective-permute-done.11.early_far, bf16[1024,768]{1,0:T(8,128)(2,1)} %copy-done.1, bf16[1024,768]{1,0:T(8,128)(2,1)} %collective-permute-done.12.late_far, ...), custom_call_target="tpu_custom_call" | custom-call | flops 1 | bytes 1 | tf_op jit(solution)/shard_map/contract/pallas_call | solution.py:222
  76.8 3.4 %collective-permute-start.17 = (bf16[2,512,128]{2,1,0:T(8,128)(2,1)}, bf16[2,512,128]{2,1,0:T(8,128)(2,1)S(1)}, u32[]{:S(2)}, u32[]{:S(2)}) collective-permute-start(bf16[2,512,128]{2,1,0:T(8,128)(2,1)} %get-tuple-element.86), channel_id=1, source_target_pairs={{0,16},{16,0},{1,17},{17,1},{2,18},{18,2},{3,19},{19,3},{4,20},{20... | collective-permute-start | bytes 786440 | tf_op jit(solution)/shard_map/ppermute | solution.py:24
  80.2 6.9 %contract.6 = (f32[2,512,128]{2,1,0:T(8,128)}, bf16[2,512,128]{2,1,0:T(8,128)(2,1)}) custom-call(s32[1]{0:T(128)} %bitcast.place, bf16[1024,768]{1,0:T(8,128)(2,1)} %copy-done, bf16[1024,768]{1,0:T(8,128)(2,1)} %collective-permute-done.11.early_far, bf16[1024,768]{1,0:T(8,128)(2,1)} %copy-done.1, bf16[1024,768]{1,0:T(8,128)(2,1)} %collective-permute-done.12.late_far, ...), custom_call_target="tpu_custom_call" | custom-call | flops 1 | bytes 1 | tf_op jit(solution)/shard_map/contract/pallas_call | solution.py:222
  88.4 2.6 %collective-permute-start.16 = (bf16[768,384]{1,0:T(8,128)(2,1)S(1)}, bf16[768,384]{1,0:T(8,128)(2,1)S(1)}, u32[]{:S(2)}, u32[]{:S(2)}) collective-permute-start(bf16[768,384]{1,0:T(8,128)(2,1)S(1)} %get-tuple-element.85), channel_id=1, source_target_pairs={{0,96},{32,0},{64,32},{96,64},{1,97},{33,1},{65,33},{97,65},{2,98}... | collective-permute-start | bytes 1769480 | tf_op jit(solution)/shard_map/ppermute | solution.py:20
  91.1 7.2 %contract.7 = (f32[2,512,256]{2,1,0:T(8,128)}, bf16[2,512,256]{2,1,0:T(8,128)(2,1)}) custom-call(s32[1]{0:T(128)} %bitcast.place, bf16[1024,768]{1,0:T(8,128)(2,1)} %copy-done, bf16[1024,768]{1,0:T(8,128)(2,1)} %collective-permute-done.11.early_far, bf16[1024,768]{1,0:T(8,128)(2,1)} %copy-done.1, bf16[1024,768]{1,0:T(8,128)(2,1)} %collective-permute-done.12.late_far, ...), custom_call_target="tpu_custom_call" | custom-call | flops 1 | bytes 1 | tf_op jit(solution)/shard_map/contract/pallas_call | solution.py:222
  98.3 3.0 %collective-permute-start.20 = (bf16[2,512,256]{2,1,0:T(8,128)(2,1)}, bf16[2,512,256]{2,1,0:T(8,128)(2,1)}, u32[]{:S(2)}, u32[]{:S(2)}) collective-permute-start(bf16[2,512,256]{2,1,0:T(8,128)(2,1)} %get-tuple-element.88), channel_id=1, source_target_pairs={{0,16},{16,0},{1,17},{17,1},{2,18},{18,2},{3,19},{19,3},{4,20},{20... | collective-permute-start | bytes 1572872 | tf_op jit(solution)/shard_map/ppermute | solution.py:24
  105.0 1.8 %payload.7 = (bf16[768,128]{1,0:T(8,128)(2,1)}, bf16[768,128]{1,0:T(8,128)(2,1)}) custom-call(bf16[768,384]{1,0:T(8,128)(2,1)} %copy-done.14, bf16[768,384]{1,0:T(8,128)(2,1)} %copy-done.15), custom_call_target="tpu_custom_call" | custom-call | flops 1 | bytes 1 | tf_op jit(solution)/shard_map/payload/pallas_call | solution.py:121
  106.8 2.7 %collective-permute-start.19 = (bf16[768,128]{1,0:T(8,128)(2,1)}, bf16[768,128]{1,0:T(8,128)(2,1)S(1)}, u32[]{:S(2)}, u32[]{:S(2)}) collective-permute-start(bf16[768,128]{1,0:T(8,128)(2,1)} %get-tuple-element.92), channel_id=1, source_target_pairs={{0,96},{32,0},{64,32},{96,64},{1,97},{33,1},{65,33},{97,65},{2,98}... | collective-permute-start | bytes 589832 | tf_op jit(solution)/shard_map/ppermute | solution.py:20
  109.5 7.2 %contract.8 = (f32[2,512,256]{2,1,0:T(8,128)}, bf16[2,512,256]{2,1,0:T(8,128)(2,1)}) custom-call(s32[1]{0:T(128)} %bitcast.place, bf16[1024,768]{1,0:T(8,128)(2,1)} %copy-done, bf16[1024,768]{1,0:T(8,128)(2,1)} %collective-permute-done.11.early_far, bf16[1024,768]{1,0:T(8,128)(2,1)} %copy-done.1, bf16[1024,768]{1,0:T(8,128)(2,1)} %collective-permute-done.12.late_far, ...), custom_call_target="tpu_custom_call" | custom-call | flops 1 | bytes 1 | tf_op jit(solution)/shard_map/contract/pallas_call | solution.py:222
  116.7 2.7 %collective-permute-start.25 = (bf16[2,512,256]{2,1,0:T(8,128)(2,1)}, bf16[2,512,256]{2,1,0:T(8,128)(2,1)S(1)}, u32[]{:S(2)}, u32[]{:S(2)}) collective-permute-start(bf16[2,512,256]{2,1,0:T(8,128)(2,1)} %get-tuple-element.93), channel_id=1, source_target_pairs={{0,16},{16,0},{1,17},{17,1},{2,18},{18,2},{3,19},{19,3},{4,20},{20... | collective-permute-start | bytes 1572872 | tf_op jit(solution)/shard_map/ppermute | solution.py:24
  120.2 7.3 %contract.9 = (f32[2,512,256]{2,1,0:T(8,128)}, bf16[2,512,256]{2,1,0:T(8,128)(2,1)}) custom-call(s32[1]{0:T(128)} %bitcast.place, bf16[1024,768]{1,0:T(8,128)(2,1)} %copy-done, bf16[1024,768]{1,0:T(8,128)(2,1)} %collective-permute-done.11.early_far, bf16[1024,768]{1,0:T(8,128)(2,1)} %copy-done.1, bf16[1024,768]{1,0:T(8,128)(2,1)} %collective-permute-done.12.late_far, ...), custom_call_target="tpu_custom_call" | custom-call | flops 1 | bytes 1 | tf_op jit(solution)/shard_map/contract/pallas_call | solution.py:222
  129.8 2.2 %collective-permute-start.27 = (bf16[512,256]{1,0:T(8,128)(2,1)S(1)}, bf16[512,256]{1,0:T(8,128)(2,1)S(1)}, u32[]{:S(2)}, u32[]{:S(2)}) collective-permute-start(bf16[512,256]{1,0:T(8,128)(2,1)S(1)} %get-tuple-element.124), channel_id=1, source_target_pairs={{0,16},{16,0},{1,17},{17,1},{2,18},{18,2},{3,19},{19,3},{4,20},{20... | collective-permute-start | bytes 786440 | tf_op jit(solution)/shard_map/ppermute | solution.py:24
  133.6 6.9 %collective-permute-done.23 = bf16[2,512,256]{2,1,0:T(8,128)(2,1)S(1)} collective-permute-done((bf16[2,512,256]{2,1,0:T(8,128)(2,1)}, bf16[2,512,256]{2,1,0:T(8,128)(2,1)S(1)}, u32[]{:S(2)}, u32[]{:S(2)}) %collective-permute-start.23) | collective-permute-done | bytes 524320 | tf_op jit(solution)/shard_map/ppermute | solution.py:24
  140.9 6.4 %collective-permute-start.28 = (f32[256,1024]{1,0:T(8,128)S(1)}, f32[256,1024]{1,0:T(8,128)S(1)}, u32[]{:S(2)}, u32[]{:S(2)}) collective-permute-start(f32[256,1024]{1,0:T(8,128)S(1)} %get-tuple-element.114), channel_id=1, source_target_pairs={{0,8},{8,0},{1,9},{9,1},{2,10},{10,2},{3,11},{11,3},{4,12},{12,4},... | collective-permute-start | bytes 3145736 | tf_op jit(solution)/shard_map/ppermute | solution.py:24
  148.1 2.1 %collective-permute-start.26 = (bf16[512,256]{1,0:T(8,128)(2,1)S(1)}, bf16[512,256]{1,0:T(8,128)(2,1)S(1)}, u32[]{:S(2)}, u32[]{:S(2)}) collective-permute-start(bf16[512,256]{1,0:T(8,128)(2,1)S(1)} %get-tuple-element.122), channel_id=1, source_target_pairs={{0,16},{16,0},{1,17},{17,1},{2,18},{18,2},{3,19},{19,3},{4,20},{20... | collective-permute-start | bytes 786440 | tf_op jit(solution)/shard_map/ppermute | solution.py:24
  151.6 4.0 %collective-permute-done.26 = bf16[512,256]{1,0:T(8,128)(2,1)S(1)} collective-permute-done((bf16[512,256]{1,0:T(8,128)(2,1)S(1)}, bf16[512,256]{1,0:T(8,128)(2,1)S(1)}, u32[]{:S(2)}, u32[]{:S(2)}) %collective-permute-start.26) | collective-permute-done | bytes 262176 | tf_op jit(solution)/shard_map/ppermute | solution.py:24
  157.7 3.5 %collective-permute-done.24 = bf16[512,256]{1,0:T(8,128)(2,1)S(1)} collective-permute-done((bf16[512,256]{1,0:T(8,128)(2,1)S(1)}, bf16[512,256]{1,0:T(8,128)(2,1)S(1)}, u32[]{:S(2)}, u32[]{:S(2)}) %collective-permute-start.24) | collective-permute-done | bytes 262176 | tf_op jit(solution)/shard_map/ppermute | solution.py:24
  164.4 2.9 %collective-permute-start.29 = (bf16[256,1024]{1,0:T(8,128)(2,1)S(1)}, bf16[256,1024]{1,0:T(8,128)(2,1)S(1)}, u32[]{:S(2)}, u32[]{:S(2)}) collective-permute-start(bf16[256,1024]{1,0:T(8,128)(2,1)S(1)} %natural.3), channel_id=1, source_target_pairs={{0,8},{8,0},{1,9},{9,1},{2,10},{10,2},{3,11},{11,3},{4,12},{12,4},... | collective-permute-start | bytes 1572872 | tf_op jit(solution)/shard_map/ppermute | solution.py:24
  (122 shorter events, 36.0 us)
Async XLA Ops:
  2.6 11.5 %collective-permute-start.1 = (bf16[384,1024]{1,0:T(8,128)(2,1)}, bf16[384,1024]{1,0:T(8,128)(2,1)S(1)}, u32[]{:S(2)}, u32[]{:S(2)}) collective-permute-start(bf16[384,1024]{1,0:T(8,128)(2,1)} %partner_columns.1), channel_id=1, source_target_pairs={{0,8},{8,0},{1,9},{9,1},{2,10},{10,2},{3,11},{11,3},{4,12},{12,4},... | collective-permute-start | bytes 2359304 | tf_op jit(solution)/shard_map/ppermute | solution.py:24
  4.0 15.1 %collective-permute-start = (bf16[384,512]{1,0:T(8,128)(2,1)}, bf16[384,512]{1,0:T(8,128)(2,1)S(1)}, u32[]{:S(2)}, u32[]{:S(2)}) collective-permute-start(bf16[384,512]{1,0:T(8,128)(2,1)} %param.4), channel_id=1, source_target_pairs={{0,0},{2,32},{4,64},{6,96},{32,2},{34,34},{36,66},{38,98},{64,4},{... | collective-permute-start | bytes 1179656 | tf_op jit(solution)/shard_map/ppermute | solution.py:28
  19.1 36.1 %copy-start.8 = (bf16[768,256]{1,0:T(8,128)(2,1)}, bf16[768,256]{1,0:T(8,128)(2,1)S(1)}, u32[]{:S(2)}) copy-start(bf16[768,256]{1,0:T(8,128)(2,1)S(1)} %get-tuple-element.80.own) | copy-start | bytes 1179652
  19.1 46.7 %copy-start.11 = (bf16[768,256]{1,0:T(8,128)(2,1)}, bf16[768,256]{1,0:T(8,128)(2,1)S(1)}, u32[]{:S(2)}) copy-start(bf16[768,256]{1,0:T(8,128)(2,1)S(1)} %get-tuple-element.76.refs_0_.own) | copy-start | bytes 1179652
  19.1 13.9 %collective-permute-start.2 = (bf16[384,512]{1,0:T(8,128)(2,1)S(1)}, bf16[384,512]{1,0:T(8,128)(2,1)S(1)}, u32[]{:S(2)}, u32[]{:S(2)}) collective-permute-start(bf16[384,512]{1,0:T(8,128)(2,1)S(1)} %collective-permute-done), channel_id=1, source_target_pairs={{0,1},{1,0},{2,3},{3,2},{4,5},{5,4},{6,7},{7,6},{8,9},{9,8},{10,11... | collective-permute-start | bytes 1179656 | tf_op jit(solution)/shard_map/ppermute | solution.py:24
  21.0 17.3 %collective-permute-start.3 = (bf16[384,512]{1,0:T(8,128)(2,1)S(1)}, bf16[384,512]{1,0:T(8,128)(2,1)S(1)}, u32[]{:S(2)}, u32[]{:S(2)}) collective-permute-start(bf16[384,512]{1,0:T(8,128)(2,1)S(1)} %collective-permute-done), channel_id=1, source_target_pairs={{0,4},{2,6},{4,0},{6,2},{1,5},{3,7},{5,1},{7,3},{8,12},{10,14},{12... | collective-permute-start | bytes 1179656 | tf_op jit(solution)/shard_map/ppermute | solution.py:16
  30.3 14.1 %collective-permute-start.7 = (bf16[768,256]{1,0:T(8,128)(2,1)S(1)}, bf16[768,256]{1,0:T(8,128)(2,1)S(1)}, u32[]{:S(2)}, u32[]{:S(2)}) collective-permute-start(bf16[768,256]{1,0:T(8,128)(2,1)S(1)} %get-tuple-element.80.own), channel_id=1, source_target_pairs={{0,32},{32,64},{64,96},{96,0},{1,33},{33,65},{65,97},{97,1},{2,34}... | collective-permute-start | bytes 1179656 | tf_op jit(solution)/shard_map/ppermute | solution.py:20
  32.0 12.3 %collective-permute-start.8 = (bf16[768,256]{1,0:T(8,128)(2,1)S(1)}, bf16[768,256]{1,0:T(8,128)(2,1)S(1)}, u32[]{:S(2)}, u32[]{:S(2)}) collective-permute-start(bf16[768,256]{1,0:T(8,128)(2,1)S(1)} %get-tuple-element.80.own), channel_id=1, source_target_pairs={{0,96},{32,0},{64,32},{96,64},{1,97},{33,1},{65,33},{97,65},{2,98}... | collective-permute-start | bytes 1179656 | tf_op jit(solution)/shard_map/ppermute | solution.py:20
  38.3 21.8 %collective-permute-start.4 = (bf16[384,1024]{1,0:T(8,128)(2,1)S(1)}, bf16[384,1024]{1,0:T(8,128)(2,1)S(1)}, u32[]{:S(2)}, u32[]{:S(2)}) collective-permute-start(bf16[384,1024]{1,0:T(8,128)(2,1)S(1)} %constant_dynamic-update-slice_fusion.first), channel_id=1, source_target_pairs={{0,2},{2,4},{4,6},{6,0},{1,3},{3,5},{5,7},{7,1},{8,10},{10,12},{12... | collective-permute-start | bytes 2359304 | tf_op jit(solution)/shard_map/ppermute | solution.py:16
  42.2 17.9 %collective-permute-start.5 = (bf16[384,1024]{1,0:T(8,128)(2,1)S(1)}, bf16[384,1024]{1,0:T(8,128)(2,1)S(1)}, u32[]{:S(2)}, u32[]{:S(2)}) collective-permute-start(bf16[384,1024]{1,0:T(8,128)(2,1)S(1)} %constant_dynamic-update-slice_fusion.first), channel_id=1, source_target_pairs={{0,6},{2,0},{4,2},{6,4},{1,7},{3,1},{5,3},{7,5},{8,14},{10,8},{12,... | collective-permute-start | bytes 2359304 | tf_op jit(solution)/shard_map/ppermute | solution.py:16
  44.6 13.8 %collective-permute-start.9 = (bf16[768,384]{1,0:T(8,128)(2,1)S(1)}, bf16[768,384]{1,0:T(8,128)(2,1)S(1)}, u32[]{:S(2)}, u32[]{:S(2)}) collective-permute-start(bf16[768,384]{1,0:T(8,128)(2,1)S(1)} %get-tuple-element.68), channel_id=1, source_target_pairs={{0,32},{32,64},{64,96},{96,0},{1,33},{33,65},{65,97},{97,1},{2,34}... | collective-permute-start | bytes 1769480 | tf_op jit(solution)/shard_map/ppermute | solution.py:20
  45.2 13.2 %collective-permute-start.10 = (bf16[768,384]{1,0:T(8,128)(2,1)S(1)}, bf16[768,384]{1,0:T(8,128)(2,1)S(1)}, u32[]{:S(2)}, u32[]{:S(2)}) collective-permute-start(bf16[768,384]{1,0:T(8,128)(2,1)S(1)} %get-tuple-element.69), channel_id=1, source_target_pairs={{0,96},{32,0},{64,32},{96,64},{1,97},{33,1},{65,33},{97,65},{2,98}... | collective-permute-start | bytes 1769480 | tf_op jit(solution)/shard_map/ppermute | solution.py:20
  47.5 7.6 %collective-permute-start.6 = (bf16[384,512]{1,0:T(8,128)(2,1)S(1)}, bf16[384,512]{1,0:T(8,128)(2,1)S(1)}, u32[]{:S(2)}, u32[]{:S(2)}) collective-permute-start(bf16[384,512]{1,0:T(8,128)(2,1)S(1)} %collective-permute-done.3), channel_id=1, source_target_pairs={{0,1},{1,0},{2,3},{3,2},{4,5},{5,4},{6,7},{7,6},{8,9},{9,8},{10,11... | collective-permute-start | bytes 1179656 | tf_op jit(solution)/shard_map/ppermute | solution.py:24
  60.2 9.8 %collective-permute-start.11 = (bf16[1024,768]{1,0:T(8,128)(2,1)S(1)}, bf16[1024,768]{1,0:T(8,128)(2,1)}, u32[]{:S(2)}, u32[]{:S(2)}) collective-permute-start(bf16[1024,768]{1,0:T(8,128)(2,1)S(1)} %rotate_in.2.early), channel_id=1, source_target_pairs={{0,8},{8,0},{1,9},{9,1},{2,10},{10,2},{3,11},{11,3},{4,12},{12,4},... | collective-permute-start | bytes 4718600 | tf_op jit(solution)/shard_map/ppermute | solution.py:24
  65.7 4.2 %collective-permute-start.12 = (bf16[1024,768]{1,0:T(8,128)(2,1)S(1)}, bf16[1024,768]{1,0:T(8,128)(2,1)}, u32[]{:S(2)}, u32[]{:S(2)}) collective-permute-start(bf16[1024,768]{1,0:T(8,128)(2,1)S(1)} %rotate_in.3.late), channel_id=1, source_target_pairs={{0,8},{8,0},{1,9},{9,1},{2,10},{10,2},{3,11},{11,3},{4,12},{12,4},... | collective-permute-start | bytes 4718600 | tf_op jit(solution)/shard_map/ppermute | solution.py:24
  67.3 19.9 %collective-permute-start.13 = (bf16[768,384]{1,0:T(8,128)(2,1)}, bf16[768,384]{1,0:T(8,128)(2,1)}, u32[]{:S(2)}, u32[]{:S(2)}) collective-permute-start(bf16[768,384]{1,0:T(8,128)(2,1)} %get-tuple-element.77), channel_id=1, source_target_pairs={{0,32},{32,64},{64,96},{96,0},{1,33},{33,65},{65,97},{97,1},{2,34}... | collective-permute-start | bytes 1769480 | tf_op jit(solution)/shard_map/ppermute | solution.py:20
  67.3 19.9 %collective-permute-start.14 = (bf16[768,384]{1,0:T(8,128)(2,1)}, bf16[768,384]{1,0:T(8,128)(2,1)}, u32[]{:S(2)}, u32[]{:S(2)}) collective-permute-start(bf16[768,384]{1,0:T(8,128)(2,1)} %get-tuple-element.78), channel_id=1, source_target_pairs={{0,96},{32,0},{64,32},{96,64},{1,97},{33,1},{65,33},{97,65},{2,98}... | collective-permute-start | bytes 1769480 | tf_op jit(solution)/shard_map/ppermute | solution.py:20
  76.8 14.3 %collective-permute-start.17 = (bf16[2,512,128]{2,1,0:T(8,128)(2,1)}, bf16[2,512,128]{2,1,0:T(8,128)(2,1)S(1)}, u32[]{:S(2)}, u32[]{:S(2)}) collective-permute-start(bf16[2,512,128]{2,1,0:T(8,128)(2,1)} %get-tuple-element.86), channel_id=1, source_target_pairs={{0,16},{16,0},{1,17},{17,1},{2,18},{18,2},{3,19},{19,3},{4,20},{20... | collective-permute-start | bytes 786440 | tf_op jit(solution)/shard_map/ppermute | solution.py:24
  87.1 14.3 %collective-permute-start.21 = (bf16[2,512,128]{2,1,0:T(8,128)(2,1)}, bf16[2,512,128]{2,1,0:T(8,128)(2,1)S(1)}, u32[]{:S(2)}, u32[]{:S(2)}) collective-permute-start(bf16[2,512,128]{2,1,0:T(8,128)(2,1)} %get-tuple-element.81), channel_id=1, source_target_pairs={{0,16},{16,0},{1,17},{17,1},{2,18},{18,2},{3,19},{19,3},{4,20},{20... | collective-permute-start | bytes 786440 | tf_op jit(solution)/shard_map/ppermute | solution.py:24
  88.3 15.0 %collective-permute-start.15 = (bf16[768,384]{1,0:T(8,128)(2,1)S(1)}, bf16[768,384]{1,0:T(8,128)(2,1)S(1)}, u32[]{:S(2)}, u32[]{:S(2)}) collective-permute-start(bf16[768,384]{1,0:T(8,128)(2,1)S(1)} %get-tuple-element.84), channel_id=1, source_target_pairs={{0,32},{32,64},{64,96},{96,0},{1,33},{33,65},{65,97},{97,1},{2,34}... | collective-permute-start | bytes 1769480 | tf_op jit(solution)/shard_map/ppermute | solution.py:20
  88.4 14.9 %collective-permute-start.16 = (bf16[768,384]{1,0:T(8,128)(2,1)S(1)}, bf16[768,384]{1,0:T(8,128)(2,1)S(1)}, u32[]{:S(2)}, u32[]{:S(2)}) collective-permute-start(bf16[768,384]{1,0:T(8,128)(2,1)S(1)} %get-tuple-element.85), channel_id=1, source_target_pairs={{0,96},{32,0},{64,32},{96,64},{1,97},{33,1},{65,33},{97,65},{2,98}... | collective-permute-start | bytes 1769480 | tf_op jit(solution)/shard_map/ppermute | solution.py:20
  98.3 21.1 %collective-permute-start.20 = (bf16[2,512,256]{2,1,0:T(8,128)(2,1)}, bf16[2,512,256]{2,1,0:T(8,128)(2,1)}, u32[]{:S(2)}, u32[]{:S(2)}) collective-permute-start(bf16[2,512,256]{2,1,0:T(8,128)(2,1)} %get-tuple-element.88), channel_id=1, source_target_pairs={{0,16},{16,0},{1,17},{17,1},{2,18},{18,2},{3,19},{19,3},{4,20},{20... | collective-permute-start | bytes 1572872 | tf_op jit(solution)/shard_map/ppermute | solution.py:24
  102.3 17.1 %collective-permute-start.22 = (bf16[512,256]{1,0:T(8,128)(2,1)}, bf16[512,256]{1,0:T(8,128)(2,1)}, u32[]{:S(2)}, u32[]{:S(2)}) collective-permute-start(bf16[512,256]{1,0:T(8,128)(2,1)} %pad_maximum_fusion.2), channel_id=1, source_target_pairs={{0,16},{16,0},{1,17},{17,1},{2,18},{18,2},{3,19},{19,3},{4,20},{20... | collective-permute-start | bytes 786440 | tf_op jit(solution)/shard_map/ppermute | solution.py:24
  106.8 12.6 %collective-permute-start.18 = (bf16[768,128]{1,0:T(8,128)(2,1)}, bf16[768,128]{1,0:T(8,128)(2,1)S(1)}, u32[]{:S(2)}, u32[]{:S(2)}) collective-permute-start(bf16[768,128]{1,0:T(8,128)(2,1)} %get-tuple-element.91), channel_id=1, source_target_pairs={{0,32},{32,64},{64,96},{96,0},{1,33},{33,65},{65,97},{97,1},{2,34}... | collective-permute-start | bytes 589832 | tf_op jit(solution)/shard_map/ppermute | solution.py:20
  106.8 12.6 %collective-permute-start.19 = (bf16[768,128]{1,0:T(8,128)(2,1)}, bf16[768,128]{1,0:T(8,128)(2,1)S(1)}, u32[]{:S(2)}, u32[]{:S(2)}) collective-permute-start(bf16[768,128]{1,0:T(8,128)(2,1)} %get-tuple-element.92), channel_id=1, source_target_pairs={{0,96},{32,0},{64,32},{96,64},{1,97},{33,1},{65,33},{97,65},{2,98}... | collective-permute-start | bytes 589832 | tf_op jit(solution)/shard_map/ppermute | solution.py:20
  116.7 16.6 %collective-permute-start.25 = (bf16[2,512,256]{2,1,0:T(8,128)(2,1)}, bf16[2,512,256]{2,1,0:T(8,128)(2,1)S(1)}, u32[]{:S(2)}, u32[]{:S(2)}) collective-permute-start(bf16[2,512,256]{2,1,0:T(8,128)(2,1)} %get-tuple-element.93), channel_id=1, source_target_pairs={{0,16},{16,0},{1,17},{17,1},{2,18},{18,2},{3,19},{19,3},{4,20},{20... | collective-permute-start | bytes 1572872 | tf_op jit(solution)/shard_map/ppermute | solution.py:24
  127.5 13.0 %collective-permute-start.23 = (bf16[2,512,256]{2,1,0:T(8,128)(2,1)}, bf16[2,512,256]{2,1,0:T(8,128)(2,1)S(1)}, u32[]{:S(2)}, u32[]{:S(2)}) collective-permute-start(bf16[2,512,256]{2,1,0:T(8,128)(2,1)} %get-tuple-element.100), channel_id=1, source_target_pairs={{0,16},{16,0},{1,17},{17,1},{2,18},{18,2},{3,19},{19,3},{4,20},{20... | collective-permute-start | bytes 1572872 | tf_op jit(solution)/shard_map/ppermute | solution.py:24
  129.8 18.0 %collective-permute-start.27 = (bf16[512,256]{1,0:T(8,128)(2,1)S(1)}, bf16[512,256]{1,0:T(8,128)(2,1)S(1)}, u32[]{:S(2)}, u32[]{:S(2)}) collective-permute-start(bf16[512,256]{1,0:T(8,128)(2,1)S(1)} %get-tuple-element.124), channel_id=1, source_target_pairs={{0,16},{16,0},{1,17},{17,1},{2,18},{18,2},{3,19},{19,3},{4,20},{20... | collective-permute-start | bytes 786440 | tf_op jit(solution)/shard_map/ppermute | solution.py:24
  140.9 15.3 %collective-permute-start.28 = (f32[256,1024]{1,0:T(8,128)S(1)}, f32[256,1024]{1,0:T(8,128)S(1)}, u32[]{:S(2)}, u32[]{:S(2)}) collective-permute-start(f32[256,1024]{1,0:T(8,128)S(1)} %get-tuple-element.114), channel_id=1, source_target_pairs={{0,8},{8,0},{1,9},{9,1},{2,10},{10,2},{3,11},{11,3},{4,12},{12,4},... | collective-permute-start | bytes 3145736 | tf_op jit(solution)/shard_map/ppermute | solution.py:24
  148.1 7.5 %collective-permute-start.26 = (bf16[512,256]{1,0:T(8,128)(2,1)S(1)}, bf16[512,256]{1,0:T(8,128)(2,1)S(1)}, u32[]{:S(2)}, u32[]{:S(2)}) collective-permute-start(bf16[512,256]{1,0:T(8,128)(2,1)S(1)} %get-tuple-element.122), channel_id=1, source_target_pairs={{0,16},{16,0},{1,17},{17,1},{2,18},{18,2},{3,19},{19,3},{4,20},{20... | collective-permute-start | bytes 786440 | tf_op jit(solution)/shard_map/ppermute | solution.py:24
  150.6 10.6 %collective-permute-start.24 = (bf16[512,256]{1,0:T(8,128)(2,1)S(1)}, bf16[512,256]{1,0:T(8,128)(2,1)S(1)}, u32[]{:S(2)}, u32[]{:S(2)}) collective-permute-start(bf16[512,256]{1,0:T(8,128)(2,1)S(1)} %get-tuple-element.120), channel_id=1, source_target_pairs={{0,16},{16,0},{1,17},{17,1},{2,18},{18,2},{3,19},{19,3},{4,20},{20... | collective-permute-start | bytes 786440 | tf_op jit(solution)/shard_map/ppermute | solution.py:24
  164.4 4.5 %collective-permute-start.29 = (bf16[256,1024]{1,0:T(8,128)(2,1)S(1)}, bf16[256,1024]{1,0:T(8,128)(2,1)S(1)}, u32[]{:S(2)}, u32[]{:S(2)}) collective-permute-start(bf16[256,1024]{1,0:T(8,128)(2,1)S(1)} %natural.3), channel_id=1, source_target_pairs={{0,8},{8,0},{1,9},{9,1},{2,10},{10,2},{3,11},{11,3},{4,12},{12,4},... | collective-permute-start | bytes 1572872 | tf_op jit(solution)/shard_map/ppermute | solution.py:24
  (22 other events, 183.8 us)
